TPU v7x, 32 devices: a whole 2x2x4 slice. The times are simulated.
32 devices in a mesh: dp: 8 (over z, x), tensor: 4 (over y, core).
Axes of the slice: x: 2, y: 2, z: 4, core: 2. Of those that a mesh axis runs over, the one named last changes fastest.
Arguments:
- tokens: bfloat16 [16384, 768], P(('dp', 'tensor')), may hold values from -6 to 6
- cotangent: bfloat16 [16384, 768], P(('dp', 'tensor')), may hold values from -6 to 6
- w_qkv: float32 [3, 768, 768], P(None, 'dp', 'tensor'), may hold values from -0.3125 to 0.3125
- w_attn_out: float32 [768, 768], P('tensor', 'dp'), may hold values from -0.625 to 0.625
- w_in: float32 [2, 768, 1152], P(None, 'dp', 'tensor'), may hold values from -0.21875 to 0.21875
- w_mlp_out: float32 [1152, 768], P('tensor', 'dp'), may hold values from -0.1875 to 0.1875
- gains: float32 [2, 768], P(None, 'dp'), may hold values from 0.5 to 1.5
- first_qkv: float32 [3, 768, 768], P(None, 'dp', 'tensor'), may hold values from -80 to 80
- first_attn_out: float32 [768, 768], P('tensor', 'dp'), may hold values from -24 to 24
- first_in: float32 [2, 768, 1152], P(None, 'dp', 'tensor'), may hold values from -48 to 48
- first_mlp_out: float32 [1152, 768], P('tensor', 'dp'), may hold values from -56 to 56
- first_gains: float32 [2, 768], P(None, 'dp'), may hold values from -128 to 128
- second_qkv: float32 [3, 768, 768], P(None, 'dp', 'tensor'), may hold values from 334.2336 to 1336.9344
- second_attn_out: float32 [768, 768], P('tensor', 'dp'), may hold values from 30.14656 to 120.25856
- second_in: float32 [2, 768, 1152], P(None, 'dp', 'tensor'), may hold values from 120.25856 to 481.6896
- second_mlp_out: float32 [1152, 768], P('tensor', 'dp'), may hold values from 141.23009 to 565.248
- second_gains: float32 [2, 768], P(None, 'dp'), may hold values from 752.0256 to 3008.1023
Outputs:
- output: bfloat16 [16384, 768], P(('dp', 'tensor'))
- grad_tokens: float32 [16384, 768], P(('dp', 'tensor'))
- grad_qkv: float32 [3, 768, 768], P(None, 'dp', 'tensor')
- grad_attn_out: float32 [768, 768], P('tensor', 'dp')
- grad_in: float32 [2, 768, 1152], P(None, 'dp', 'tensor')
- grad_mlp_out: float32 [1152, 768], P('tensor', 'dp')
- grad_gains: float32 [2, 768], P(None, 'dp')
- new_w_qkv: float32 [3, 768, 768], P(None, 'dp', 'tensor')
- new_w_attn_out: float32 [768, 768], P('tensor', 'dp')
- new_w_in: float32 [2, 768, 1152], P(None, 'dp', 'tensor')
- new_w_mlp_out: float32 [1152, 768], P('tensor', 'dp')
- new_gains: float32 [2, 768], P(None, 'dp')
- new_first_qkv: float32 [3, 768, 768], P(None, 'dp', 'tensor')
- new_first_attn_out: float32 [768, 768], P('tensor', 'dp')
- new_first_in: float32 [2, 768, 1152], P(None, 'dp', 'tensor')
- new_first_mlp_out: float32 [1152, 768], P('tensor', 'dp')
- new_first_gains: float32 [2, 768], P(None, 'dp')
- new_second_qkv: float32 [3, 768, 768], P(None, 'dp', 'tensor')
- new_second_attn_out: float32 [768, 768], P('tensor', 'dp')
- new_second_in: float32 [2, 768, 1152], P(None, 'dp', 'tensor')
- new_second_mlp_out: float32 [1152, 768], P('tensor', 'dp')
- new_second_gains: float32 [2, 768], P(None, 'dp')
All inputs are finite; a program needn't handle non-finite values.
Results may differ from a plain program's by a relative error of at most 0.014.
The roundings to bfloat16 on the way count: a program that leaves them out, or rounds other values in their place, can miss the bound.
Values may be sent and summed in bfloat16 or wider, within the bound.
No kernel may reach another device: no remote copies, remote signals or barrier semaphores. Data moves between devices by JAX's collectives and lax.ppermute only.
A program may use at most 128 MiB of HBM per device.

v0:
```python
import jax
import jax.numpy as jnp
from jax import lax
from jax.sharding import PartitionSpec as P

HD = 64
L = 1024
STEP = 10


eps_norm = 1e-05
rope_base = 160000.0
beta_one = 0.9
beta_two = 0.98
adam_eps = 1e-06
weight_rate = 0.02
gain_rate = 0.2
weight_decay = 0.01


def layer_norm(values, scales):
    centred = values - jnp.mean(values, axis=-1, keepdims=True)
    spread = jnp.mean(centred * centred, axis=-1, keepdims=True)
    return centred * lax.rsqrt(spread + eps_norm) * scales


def rotary(values, seq_len):
    row_count, head_count, head_width = values.shape
    half_width = head_width // 2
    frequency = rope_base ** (-(jnp.arange(half_width, dtype=jnp.float32) * 2.0 / head_width))
    position = (jnp.arange(row_count) % seq_len).astype(jnp.float32)
    angles = position[:, None] * frequency[None, :]
    angles = jnp.concatenate([angles, angles], axis=-1)[:, None, :]
    turned = jnp.concatenate([-values[..., half_width:], values[..., :half_width]], axis=-1)
    return values * jnp.cos(angles) + turned * jnp.sin(angles)


def rotate_pair(query_raw, key_raw):
    return (rotary(query_raw, L), rotary(key_raw, L))


def gated(gate_part, up_part):
    return jax.nn.gelu(gate_part, approximate=False) * up_part


def attend_forward(triple):
    queries, keys, values = triple
    length = queries.shape[0]
    span = min(512, length)
    scale = HD ** (-0.5)
    pieces = []
    totals = []
    for offset in range(0, length, span):
        query_part = queries[offset : offset + span]
        scores = (
            jnp.einsum("qhd,khd->hqk", query_part, keys, preferred_element_type=jnp.float32) * scale
        )
        row_max = jnp.max(scores, axis=-1, keepdims=True)
        log_total = jnp.log(jnp.sum(jnp.exp(scores - row_max), axis=-1, keepdims=True)) + row_max
        attn_probs = jnp.exp(scores - log_total).astype(jnp.bfloat16)
        pieces.append(
            jnp.einsum("hqk,khd->qhd", attn_probs, values, preferred_element_type=jnp.float32)
        )
        totals.append(log_total[..., 0])
    return (jnp.concatenate(pieces, axis=0), jnp.concatenate(totals, axis=1))


def attend_backward(bundle):
    queries, keys, values, grads, totals = bundle
    length = queries.shape[0]
    span = min(512, length)
    scale = HD ** (-0.5)
    key_grad = jnp.zeros(keys.shape, jnp.float32)
    value_grad = jnp.zeros(values.shape, jnp.float32)
    query_grads = []
    for offset in range(0, length, span):
        query_part = queries[offset : offset + span]
        grad_part = grads[offset : offset + span]
        scores = (
            jnp.einsum("qhd,khd->hqk", query_part, keys, preferred_element_type=jnp.float32) * scale
        )
        attn_probs = jnp.exp(scores - totals[:, offset : offset + span, None])
        value_grad = value_grad + jnp.einsum(
            "hqk,qhd->khd",
            attn_probs.astype(jnp.bfloat16),
            grad_part,
            preferred_element_type=jnp.float32,
        )
        prob_grad = jnp.einsum(
            "qhd,khd->hqk", grad_part, values, preferred_element_type=jnp.float32
        )
        inner = jnp.sum(attn_probs * prob_grad, axis=-1, keepdims=True)
        score_grad = (attn_probs * (prob_grad - inner)).astype(jnp.bfloat16)
        query_grads.append(
            jnp.einsum("hqk,khd->qhd", score_grad, keys, preferred_element_type=jnp.float32) * scale
        )
        key_grad = (
            key_grad
            + jnp.einsum("hqk,qhd->khd", score_grad, query_part, preferred_element_type=jnp.float32)
            * scale
        )
    return (jnp.concatenate(query_grads, axis=0), key_grad, value_grad)


def mlp_front(source, in_weight):
    both = jnp.einsum("td,cdf->ctf", source, in_weight, preferred_element_type=jnp.float32)
    hidden, gated_back = jax.vjp(gated, both[0], both[1])
    return (hidden.astype(jnp.bfloat16), gated_back)


def mlp_back(grad_hidden, gated_back):
    grad_gate, grad_up = gated_back(grad_hidden)
    return jnp.stack([grad_gate, grad_up]).astype(jnp.bfloat16)


def adamw(weight, grad, first, second, rate, decay):
    first_new = beta_one * first + (1.0 - beta_one) * grad
    second_new = beta_two * second + (1.0 - beta_two) * grad * grad
    step_size = (
        first_new
        / (1.0 - beta_one**STEP)
        / (jnp.sqrt(second_new / (1.0 - beta_two**STEP)) + adam_eps)
    )
    return (weight - rate * (step_size + decay * weight), first_new, second_new)


def shards(
    tokens,
    cotangent,
    w_qkv,
    w_attn_out,
    w_in,
    w_mlp_out,
    gains,
    first_qkv,
    first_attn_out,
    first_in,
    first_mlp_out,
    first_gains,
    second_qkv,
    second_attn_out,
    second_in,
    second_mlp_out,
    second_gains,
):
    qkv_low, attn_low, in_low, down_low = (
        lax.all_gather(w_qkv.astype(jnp.bfloat16), "dp", axis=1, tiled=True),
        lax.all_gather(w_attn_out.astype(jnp.bfloat16), "dp", axis=1, tiled=True),
        lax.all_gather(w_in.astype(jnp.bfloat16), "dp", axis=1, tiled=True),
        lax.all_gather(w_mlp_out.astype(jnp.bfloat16), "dp", axis=1, tiled=True),
    )
    gains_all = lax.all_gather(gains, "dp", axis=1, tiled=True)
    rows_local = tokens.shape[0]
    group_rows = rows_local * lax.axis_size("tensor")
    seq_count = group_rows // L
    heads_dev = qkv_low.shape[2] // HD
    inputs = tokens.astype(jnp.float32)
    normed_one, norm_one_back = jax.vjp(layer_norm, inputs, gains_all[0])
    normed_one = normed_one.astype(jnp.bfloat16)
    rows_one = lax.all_gather(normed_one, "tensor", axis=0, tiled=True)
    proj = jnp.einsum("td,cdn->ctn", rows_one, qkv_low, preferred_element_type=jnp.float32)
    (query_rot, key_rot), rope_back = jax.vjp(
        rotate_pair,
        proj[0].reshape(group_rows, heads_dev, HD),
        proj[1].reshape(group_rows, heads_dev, HD),
    )
    queries = query_rot.astype(jnp.bfloat16).reshape(seq_count, L, heads_dev, HD)
    keys = key_rot.astype(jnp.bfloat16).reshape(seq_count, L, heads_dev, HD)
    values = proj[2].astype(jnp.bfloat16).reshape(seq_count, L, heads_dev, HD)
    attended, totals = lax.map(attend_forward, (queries, keys, values))
    mixed = attended.reshape(group_rows, heads_dev * HD).astype(jnp.bfloat16)
    resid = inputs + lax.psum_scatter(
        jnp.dot(
            lax.slice_in_dim(mixed, 0, rows_local * lax.axis_size("tensor"), axis=0),
            attn_low,
            preferred_element_type=jnp.float32,
        ),
        "tensor",
        scatter_dimension=0,
        tiled=True,
    )
    normed_two, norm_two_back = jax.vjp(layer_norm, resid, gains_all[1])
    normed_two = normed_two.astype(jnp.bfloat16)
    rows_two = lax.all_gather(normed_two, "tensor", axis=0, tiled=True)
    hidden, gated_back = mlp_front(rows_two, in_low)
    output = (
        resid
        + lax.psum_scatter(
            jnp.dot(
                lax.slice_in_dim(hidden, 0, lax.axis_size("tensor") * rows_local, axis=0),
                down_low,
                preferred_element_type=jnp.float32,
            ).astype(jnp.bfloat16),
            "tensor",
            scatter_dimension=0,
            tiled=True,
        ).astype(jnp.float32)
    ).astype(jnp.bfloat16)
    pull_rows = lax.all_gather(cotangent, "tensor", axis=0, tiled=True)
    grad_down = jnp.einsum("tf,td->fd", hidden, pull_rows, preferred_element_type=jnp.float32)
    grad_hidden = jnp.einsum("td,fd->tf", pull_rows, down_low, preferred_element_type=jnp.float32)
    grad_both = mlp_back(grad_hidden, gated_back)
    grad_in_w = jnp.einsum("td,ctf->cdf", rows_two, grad_both, preferred_element_type=jnp.float32)
    grad_normed_two = lax.psum_scatter(
        jnp.einsum("ctf,cdf->td", grad_both, in_low, preferred_element_type=jnp.float32),
        "tensor",
        scatter_dimension=0,
        tiled=True,
    )
    grad_resid_norm, grad_gain_two = norm_two_back(grad_normed_two)
    grad_resid = cotangent.astype(jnp.float32) + grad_resid_norm
    resid_rows = lax.all_gather(grad_resid.astype(jnp.bfloat16), "tensor", axis=0, tiled=True)
    grad_attn = jnp.einsum("tn,td->nd", mixed, resid_rows, preferred_element_type=jnp.float32)
    grad_mixed = jnp.einsum(
        "td,nd->tn", resid_rows, attn_low, preferred_element_type=jnp.float32
    ).astype(jnp.bfloat16)
    grad_mixed = grad_mixed.reshape(seq_count, L, heads_dev, HD)
    grad_query, grad_key, grad_value = lax.map(
        attend_backward, (queries, keys, values, grad_mixed, totals)
    )
    query_raw_grad, key_raw_grad = rope_back(
        (grad_query.reshape(group_rows, heads_dev, HD), grad_key.reshape(group_rows, heads_dev, HD))
    )
    grad_proj = jnp.stack(
        [
            query_raw_grad.reshape(group_rows, heads_dev * HD),
            key_raw_grad.reshape(group_rows, heads_dev * HD),
            grad_value.reshape(group_rows, heads_dev * HD),
        ]
    ).astype(jnp.bfloat16)
    grad_qkv_w = jnp.einsum("td,ctn->cdn", rows_one, grad_proj, preferred_element_type=jnp.float32)
    grad_normed_one = lax.psum_scatter(
        jnp.einsum("ctn,cdn->td", grad_proj, qkv_low, preferred_element_type=jnp.float32),
        "tensor",
        scatter_dimension=0,
        tiled=True,
    )
    grad_input_norm, grad_gain_one = norm_one_back(grad_normed_one)
    grad_inputs = grad_resid + grad_input_norm
    grad_gain = jnp.stack([grad_gain_one, grad_gain_two])
    shard_qkv, shard_attn, shard_in, shard_down, shard_gain = (
        lax.psum_scatter(grad_qkv_w, "dp", scatter_dimension=1, tiled=True),
        lax.psum_scatter(grad_attn, "dp", scatter_dimension=1, tiled=True),
        lax.psum_scatter(grad_in_w, "dp", scatter_dimension=1, tiled=True),
        lax.psum_scatter(grad_down, "dp", scatter_dimension=1, tiled=True),
        lax.psum_scatter(grad_gain, "dp", scatter_dimension=1, tiled=True),
    )
    shard_gain = lax.psum(shard_gain, "tensor")
    new_qkv = adamw(w_qkv, shard_qkv, first_qkv, second_qkv, weight_rate, weight_decay)
    new_attn = adamw(
        w_attn_out, shard_attn, first_attn_out, second_attn_out, weight_rate, weight_decay
    )
    new_in = adamw(w_in, shard_in, first_in, second_in, weight_rate, weight_decay)
    new_down = adamw(
        w_mlp_out, shard_down, first_mlp_out, second_mlp_out, weight_rate, weight_decay
    )
    new_gain = adamw(gains, shard_gain, first_gains, second_gains, gain_rate, 0.0)
    return (
        output,
        grad_inputs,
        shard_qkv,
        shard_attn,
        shard_in,
        shard_down,
        shard_gain,
        new_qkv[0],
        new_attn[0],
        new_in[0],
        new_down[0],
        new_gain[0],
        new_qkv[1],
        new_attn[1],
        new_in[1],
        new_down[1],
        new_gain[1],
        new_qkv[2],
        new_attn[2],
        new_in[2],
        new_down[2],
        new_gain[2],
    )


def solution(mesh):
    return jax.shard_map(
        shards,
        mesh=mesh,
        in_specs=(
            P(("dp", "tensor"), None),
            P(("dp", "tensor"), None),
            P(None, "dp", "tensor"),
            P("tensor", "dp"),
            P(None, "dp", "tensor"),
            P("tensor", "dp"),
            P(None, "dp"),
            P(None, "dp", "tensor"),
            P("tensor", "dp"),
            P(None, "dp", "tensor"),
            P("tensor", "dp"),
            P(None, "dp"),
            P(None, "dp", "tensor"),
            P("tensor", "dp"),
            P(None, "dp", "tensor"),
            P("tensor", "dp"),
            P(None, "dp"),
        ),
        out_specs=(
            P(("dp", "tensor"), None),
            P(("dp", "tensor"), None),
            P(None, "dp", "tensor"),
            P("tensor", "dp"),
            P(None, "dp", "tensor"),
            P("tensor", "dp"),
            P(None, "dp"),
            P(None, "dp", "tensor"),
            P("tensor", "dp"),
            P(None, "dp", "tensor"),
            P("tensor", "dp"),
            P(None, "dp"),
            P(None, "dp", "tensor"),
            P("tensor", "dp"),
            P(None, "dp", "tensor"),
            P("tensor", "dp"),
            P(None, "dp"),
            P(None, "dp", "tensor"),
            P("tensor", "dp"),
            P(None, "dp", "tensor"),
            P("tensor", "dp"),
            P(None, "dp"),
        ),
        check_vma=False,
    )
```

profile of v0, /device:TPU:0, one launch (start us, length us, event | category | flops | bytes accessed | tf_op | source)
XLA Modules:
  0.0 872.9 jit_solution(8322148173901804920)
XLA Ops:
  10.2 22.5 %all-gather = f32[8,96,2]{1,2,0:T(2,128)S(1)} all-gather(f32[1,96,2]{1,2,0:T(2,128)} %bitcast.372), channel_id=1, replica_groups=mesh['dp'=8,'tensor'=4] {'dp'}, dimensions={0}, use_global_device_ids=true | all-gather | bytes 6912 | tf_op jit(solution)/shard_map/all_gather | solution.py:152
  36.1 35.2 %all_gather.29 = bf16[3,768,192]{2,0,1:T(4,128)(2,1)S(1)} all-gather(bf16[3,96,192]{2,0,1:T(4,128)(2,1)S(1)} %copy.134), channel_id=1, replica_groups=mesh['dp'=8,'tensor'=4] {'dp'}, dimensions={1}, use_global_device_ids=true | all-gather | bytes 995328 | tf_op jit(solution)/shard_map/all_gather | solution.py:147
  72.2 31.2 %all_gather.30 = bf16[192,768]{0,1:T(8,128)(2,1)S(1)} all-gather(bf16[192,96]{0,1:T(8,128)(2,1)S(1)} %copy.140), channel_id=1, replica_groups=mesh['dp'=8,'tensor'=4] {'dp'}, dimensions={1}, use_global_device_ids=true | all-gather | bytes 331776 | tf_op jit(solution)/shard_map/all_gather | solution.py:148
  103.5 8.2 fusion.129
  139.7 4.1 fusion.112
  145.2 20.2 %while.26 = (s32[]{:T(128)}, bf16[2,1024,3,64]{1,3,2,0:T(8,128)(2,1)S(1)}, f32[2,3,1024]{2,1,0:T(4,128)}, bf16[2,1024,3,64]{1,3,2,0:T(8,128)(2,1)S(1)}, bf16[2,1...) while((s32[]{:T(128)}, ...), condition=%wide.region_7.8_spmd, body=%wide.region_2.7_spmd.sunk | while | flops 831258624 | bytes 41015936 | solution.py:170
  171.9 57.7 %reduce-scatter.20.cloned.1.call-done = f32[512,768]{1,0:T(8,128)} async-done(((f32[2048,768]{1,0:T(8,128)}), f32[512,768]{1,0:T(8,128)}) %reduce-scatter.20.cloned.1.call-update) | async-done | bytes 1572880 | tf_op jit(solution)/shard_map/reduce_scatter | solution.py:172
  235.8 34.1 %all_gather.33 = bf16[288,768]{0,1:T(8,128)(2,1)} all-gather(bf16[288,96]{0,1:T(8,128)(2,1)} %copy.143), channel_id=1, replica_groups=mesh['dp'=8,'tensor'=4] {'dp'}, dimensions={1}, use_global_device_ids=true | all-gather | bytes 497664 | tf_op jit(solution)/shard_map/all_gather | solution.py:150
  270.0 36.1 %all_gather.32 = bf16[2,768,288]{2,0,1:T(2,128)(2,1)} all-gather(bf16[2,96,288]{2,0,1:T(2,128)(2,1)S(1)} %copy.205), channel_id=1, replica_groups=mesh['dp'=8,'tensor'=4] {'dp'}, dimensions={1}, use_global_device_ids=true | all-gather | bytes 995328 | tf_op jit(solution)/shard_map/all_gather | solution.py:149
  306.0 4.6 fusion.159
  310.6 4.5 convolution_bitcast_fusion.2
  315.1 5.6 fusion.120
  323.9 4.7 convolution_bitcast_fusion.1
  328.8 4.9 convolution_convert_fusion
  333.8 53.5 %reduce-scatter.24.cloned.1.call-done = f32[512,768]{1,0:T(8,128)} async-done(((f32[2048,768]{1,0:T(8,128)}), f32[512,768]{1,0:T(8,128)}) %reduce-scatter.24.cloned.1.call-update) | async-done | bytes 1572880 | tf_op jit(solution)/shard_map/reduce_scatter | solution.py:204
  390.4 37.2 %reduce-scatter.22.cloned.1.call-done = bf16[512,768]{1,0:T(8,128)(2,1)} async-done(((bf16[2048,768]{1,0:T(8,128)(2,1)}), bf16[512,768]{1,0:T(8,128)(2,1)}) %reduce-scatter.22.cloned.1.call-update) | async-done | bytes 786448 | tf_op jit(solution)/shard_map/reduce_scatter | solution.py:188
  433.7 4.8 convolution_bitcast_fusion.3
  441.3 5.7 fusion.113
  447.0 5.1 copy.173
  456.1 5.8 all-gather.12.cloned.1.call-done
  467.6 110.4 %while.27 = (s32[]{:T(128)}, f32[2,1024,3,64]{1,0,3,2:T(2,128)}, f32[2,1024,3,64]{1,0,3,2:T(2,128)}, bf16[2,1024,3,64]{1,3,2,0:T(8,128)(2,1)}, bf16[2,1024,3,64]...) while((s32[]{:T(128)}, f32[2,1024,3,64]{1,0,3,2:T(2,128)}, ...), condition=%wide.region_18.19_spmd, body=%wide.region_15.18_spmd.sunk | while | flops 2051994624 | bytes 124375328 | solution.py:218
  494.2 14.3 %dynamic_update_slice.28 = f32[2,1024,3,64]{1,0,3,2:T(2,128)} dynamic-update-slice(f32[2,1024,3,64]{1,0,3,2:T(2,128)} %get-tuple-element.513, f32[1,1024,3,64]{1,0,3,2:T(1,128)S(1)} %copy.208, s32[]{:T(128)S(6)} %copy.228, s32[]{:T(128)} %constant.70.clone.1..sunk.1, s32[]{:T(128)} %constant.70.clone.1..sunk.1, s32[]{:T(128)} %constant.70.clone.1..sunk.1) | dynamic-update-slice | bytes 1572868 | tf_op jit(solution)/shard_map/while/body/jit(dynamic_update_index_in_dim)/dynamic_update_slice | solution.py:170
  508.5 14.3 %dynamic_update_slice.29 = f32[2,1024,3,64]{1,0,3,2:T(2,128)} dynamic-update-slice(f32[2,1024,3,64]{1,0,3,2:T(2,128)} %get-tuple-element.514, f32[1,1024,3,64]{1,0,3,2:T(1,128)S(1)} %copy.209, s32[]{:T(128)S(6)} %copy.228, s32[]{:T(128)} %constant.70.clone.1..sunk.1, s32[]{:T(128)} %constant.70.clone.1..sunk.1, s32[]{:T(128)} %constant.70.clone.1..sunk.1) | dynamic-update-slice | bytes 1572868 | tf_op jit(solution)/shard_map/while/body/jit(dynamic_update_index_in_dim)/dynamic_update_slice | solution.py:170
  549.2 14.3 %dynamic_update_slice.28 = f32[2,1024,3,64]{1,0,3,2:T(2,128)} dynamic-update-slice(f32[2,1024,3,64]{1,0,3,2:T(2,128)} %get-tuple-element.513, f32[1,1024,3,64]{1,0,3,2:T(1,128)S(1)} %copy.208, s32[]{:T(128)S(6)} %copy.228, s32[]{:T(128)} %constant.70.clone.1..sunk.1, s32[]{:T(128)} %constant.70.clone.1..sunk.1, s32[]{:T(128)} %constant.70.clone.1..sunk.1) | dynamic-update-slice | bytes 1572868 | tf_op jit(solution)/shard_map/while/body/jit(dynamic_update_index_in_dim)/dynamic_update_slice | solution.py:170
  563.6 14.3 %dynamic_update_slice.29 = f32[2,1024,3,64]{1,0,3,2:T(2,128)} dynamic-update-slice(f32[2,1024,3,64]{1,0,3,2:T(2,128)} %get-tuple-element.514, f32[1,1024,3,64]{1,0,3,2:T(1,128)S(1)} %copy.209, s32[]{:T(128)S(6)} %copy.228, s32[]{:T(128)} %constant.70.clone.1..sunk.1, s32[]{:T(128)} %constant.70.clone.1..sunk.1, s32[]{:T(128)} %constant.70.clone.1..sunk.1) | dynamic-update-slice | bytes 1572868 | tf_op jit(solution)/shard_map/while/body/jit(dynamic_update_index_in_dim)/dynamic_update_slice | solution.py:170
  583.4 4.5 convolution_bitcast_fusion.4
  610.6 7.2 convolution_bitcast_fusion
  626.7 37.3 %reduce-scatter.30.cloned.1.call-done = f32[96,192]{1,0:T(8,128)} async-done(((f32[768,192]{1,0:T(8,128)}), f32[96,192]{1,0:T(8,128)}) %reduce-scatter.30.cloned.1.call-update) | async-done | bytes 73744
  665.7 68.1 %reduce-scatter.28.cloned.1.call-done = f32[96,576]{1,0:T(8,128)} async-done(((f32[768,576]{1,0:T(8,128)}), f32[96,576]{1,0:T(8,128)}) %reduce-scatter.28.cloned.1.call-update) | async-done | bytes 221200
  738.8 54.8 %reduce-scatter.26.cloned.1.call-done = f32[512,768]{1,0:T(8,128)} async-done(((f32[2048,768]{1,0:T(8,128)}), f32[512,768]{1,0:T(8,128)}) %reduce-scatter.26.cloned.1.call-update) | async-done | bytes 1572880 | tf_op jit(solution)/shard_map/reduce_scatter | solution.py:232
  800.6 58.2 %reduce-scatter.36.cloned.1.call-done = f32[96,2]{1,0:T(8,128)} async-done(((f32[768,2]{1,0:T(8,128)}), f32[96,2]{1,0:T(8,128)}) %reduce-scatter.36.cloned.1.call-update) | async-done | bytes 784
  859.7 5.6 psum.7
  (304 shorter events, 198.4 us)
Async XLA Ops:
  7.2 28.7 %copy-start.15 = (f32[3,96,192]{2,1,0:T(8,128)S(1)}, f32[3,96,192]{2,1,0:T(8,128)}, u32[]{:S(2)}) copy-start(f32[3,96,192]{2,1,0:T(8,128)} %param.23) | copy-start | bytes 663556
  7.2 104.5 %all-gather.6.cloned.1.call-start = ((), (), s32[]{:S(2)}) async-start(), calls=%async_computation.9 | async-start | bytes 3932160 | tf_op jit(solution)/shard_map/all_gather | solution.py:160
  35.7 193.9 %reduce-scatter.20.cloned.1.call-start = ((), (), s32[]{:S(2)}) async-start(), calls=%async_computation.10 | async-start | bytes 7864320 | tf_op jit(solution)/shard_map/reduce_scatter | solution.py:172
  72.2 43.5 %copy-start.20 = (bf16[3,768,192]{1,2,0:T(8,128)(2,1)}, bf16[3,768,192]{1,2,0:T(8,128)(2,1)S(1)}, u32[]{:S(2)}) copy-start(bf16[3,768,192]{1,2,0:T(8,128)(2,1)S(1)} %copy.135) | copy-start | bytes 2654212
  72.2 43.5 %copy-start.51 = (f32[32]{0:T(128)}, f32[32]{0:T(128)S(1)}, u32[]{:S(2)}) copy-start(f32[32]{0:T(128)S(1)} %negate_power_fusion) | copy-start | bytes 388
  171.1 134.9 %all-gather.10.cloned.1.call-start = ((), (), s32[]{:S(2)}) async-start(), calls=%async_computation.13 | async-start | bytes 3932160 | tf_op jit(solution)/shard_map/all_gather | solution.py:199
  171.8 138.8 %all-gather.8.cloned.1.call-start = ((), (), s32[]{:S(2)}) async-start(), calls=%async_computation.11 | async-start | bytes 3932160 | tf_op jit(solution)/shard_map/all_gather | solution.py:184
  232.9 154.3 %reduce-scatter.24.cloned.1.call-start = ((), (), s32[]{:S(2)}) async-start(), calls=%async_computation.14 | async-start | bytes 7864320 | tf_op jit(solution)/shard_map/reduce_scatter | solution.py:204
  328.7 98.9 %reduce-scatter.22.cloned.1.call-start = ((), (), s32[]{:S(2)}) async-start(), calls=%async_computation.12 | async-start | bytes 3932160 | tf_op jit(solution)/shard_map/reduce_scatter | solution.py:188
  333.7 128.2 %all-gather.12.cloned.1.call-start = ((), (), s32[]{:S(2)}) async-start(), calls=%async_computation.15 | async-start | bytes 3932160 | tf_op jit(solution)/shard_map/all_gather | solution.py:212
  433.2 186.5 %reduce-scatter.34.cloned.1.call-start = ((), (), s32[]{:S(2)}) async-start(), calls=%async_computation.20 | async-start | bytes 1327104
  438.5 183.2 %reduce-scatter.32.cloned.1.call-start = ((), (), s32[]{:S(2)}) async-start(), calls=%async_computation.19 | async-start | bytes 2211840
  456.0 207.9 %reduce-scatter.30.cloned.1.call-start = ((), (), s32[]{:S(2)}) async-start(), calls=%async_computation.18 | async-start | bytes 884736
  493.4 29.5 %copy-start.3 = (bf16[2,1024,3,64]{1,3,2,0:T(8,128)(2,1)S(1)}, bf16[2,1024,3,64]{1,3,2,0:T(8,128)(2,1)}, u32[]{:S(2)}) copy-start(bf16[2,1024,3,64]{1,3,2,0:T(8,128)(2,1)} %copy-done.2) | copy-start | bytes 2359300 | tf_op jit(solution)/shard_map/while
  548.4 29.5 %copy-start.3 = (bf16[2,1024,3,64]{1,3,2,0:T(8,128)(2,1)S(1)}, bf16[2,1024,3,64]{1,3,2,0:T(8,128)(2,1)}, u32[]{:S(2)}) copy-start(bf16[2,1024,3,64]{1,3,2,0:T(8,128)(2,1)} %copy-done.2) | copy-start | bytes 2359300 | tf_op jit(solution)/shard_map/while
  587.9 145.9 %reduce-scatter.28.cloned.1.call-start = ((), (), s32[]{:S(2)}) async-start(), calls=%async_computation.17 | async-start | bytes 2211840
  610.3 183.3 %reduce-scatter.26.cloned.1.call-start = ((), (), s32[]{:S(2)}) async-start(), calls=%async_computation.16 | async-start | bytes 7864320 | tf_op jit(solution)/shard_map/reduce_scatter | solution.py:232
  617.9 240.9 %reduce-scatter.36.cloned.1.call-start = ((), (), s32[]{:S(2)}) async-start(), calls=%async_computation.21 | async-start | bytes 442368
  623.6 41.3 %copy-start.27 = (f32[192,96]{1,0:T(8,128)S(1)}, f32[192,96]{1,0:T(8,128)}, u32[]{:S(2)}) copy-start(f32[192,96]{1,0:T(8,128)} %param.24) | copy-start | bytes 221188
  623.6 41.3 %copy-start.38 = (f32[192,96]{1,0:T(8,128)S(1)}, f32[192,96]{1,0:T(8,128)}, u32[]{:S(2)}) copy-start(f32[192,96]{1,0:T(8,128)} %param.29) | copy-start | bytes 221188
  623.6 41.3 %copy-start.39 = (f32[192,96]{1,0:T(8,128)S(1)}, f32[192,96]{1,0:T(8,128)}, u32[]{:S(2)}) copy-start(f32[192,96]{1,0:T(8,128)} %param.34) | copy-start | bytes 221188
  664.9 71.2 %copy-start.28 = (f32[192,96]{1,0:T(8,128)}, f32[192,96]{1,0:T(8,128)S(1)}, u32[]{:S(2)}) copy-start(f32[192,96]{1,0:T(8,128)S(1)} %copy.172) | copy-start | bytes 221188
  735.7 57.9 %copy-start.4 = (bf16[512,768]{1,0:T(8,128)(2,1)S(1)}, bf16[512,768]{1,0:T(8,128)(2,1)}, u32[]{:S(2)}) copy-start(bf16[512,768]{1,0:T(8,128)(2,1)} %param.21) | copy-start | bytes 2359300
  735.7 57.9 %copy-start.37 = (f32[768]{0:T(1024)S(1)}, f32[768]{0:T(1024)}, u32[]{:S(2)}) copy-start(f32[768]{0:T(1024)} %copy-done.36) | copy-start | bytes 9220
  735.7 57.9 %copy-start.41 = (f32[512]{0:T(512)S(1)}, f32[512]{0:T(512)}, u32[]{:S(2)}) copy-start(f32[512]{0:T(512)} %copy-done.40) | copy-start | bytes 6148
  736.1 59.4 %copy-start.47 = (f32[512]{0:T(512)S(1)}, f32[512]{0:T(512)}, u32[]{:S(2)}) copy-start(f32[512]{0:T(512)} %copy-done.46) | copy-start | bytes 6148
  736.1 59.4 %copy-start.43 = (f32[512]{0:T(512)S(1)}, f32[512]{0:T(512)}, u32[]{:S(2)}) copy-start(f32[512]{0:T(512)} %copy-done.42) | copy-start | bytes 6148
  738.8 58.6 %copy-start.9 = (bf16[512,768]{1,0:T(8,128)(2,1)S(1)}, bf16[512,768]{1,0:T(8,128)(2,1)}, u32[]{:S(2)}) copy-start(bf16[512,768]{1,0:T(8,128)(2,1)} %param.22) | copy-start | bytes 2359300
  738.8 58.6 %copy-start.45 = (f32[512]{0:T(512)S(1)}, f32[512]{0:T(512)}, u32[]{:S(2)}) copy-start(f32[512]{0:T(512)} %copy-done.44) | copy-start | bytes 6148
  797.4 68.0 %copy-start.49 = (f32[2,96]{1,0:T(2,128)S(1)}, f32[2,96]{1,0:T(2,128)}, u32[]{:S(2)}) copy-start(f32[2,96]{1,0:T(2,128)} %param.27) | copy-start | bytes 2308
  797.4 67.9 %copy-start.53 = (f32[2,96]{1,0:T(2,128)S(1)}, f32[2,96]{1,0:T(2,128)}, u32[]{:S(2)}) copy-start(f32[2,96]{1,0:T(2,128)} %param.32) | copy-start | bytes 2308
  797.4 67.9 %copy-start.54 = (f32[2,96]{1,0:T(2,128)S(1)}, f32[2,96]{1,0:T(2,128)}, u32[]{:S(2)}) copy-start(f32[2,96]{1,0:T(2,128)} %param.37) | copy-start | bytes 2308
  (41 other events, 212.5 us)
Sparse Core Ops, SparseCore 0:
  35.8 25.8 all-gather.5
  171.2 58.3 reduce-scatter.19
  231.2 28.5 all-gather.9
  261.9 28.5 all-gather.7
  328.8 58.3 reduce-scatter.23
  389.7 37.9 reduce-scatter.21
  433.3 28.5 all-gather.11
  465.7 64.0 reduce-scatter.33
  533.7 65.6 reduce-scatter.31
  602.5 61.3 reduce-scatter.29
  667.8 65.9 reduce-scatter.27
  736.2 57.3 reduce-scatter.25
  797.5 61.2 reduce-scatter.35
where the time goes:
time: 888 us; the launch traced here: 873 us
  waiting for transfers between devices  373 us (42%)
  blocking collectives  165 us (19%)
  local copies, waits for them, and re-layouts  136 us (15%)
  matrix products  111 us (12%)
  other arithmetic  70.4 us (8%)
  between operations  15.2 us (2%)
    unnamed x18, waiting for transfers between devices  164 us
    dynamic_update_slice x8, local copies, waits for them, and re-layouts, shards(): attended, totals = lax.map(attend_forward, (queries, keys, values))  60.5 us
    reduce_scatter x1, waiting for transfers between devices, shards(): lax.psum_scatter(jnp.dot(lax.slice_in_dim(mixed, 0, rows_local * lax.axis...  57.7 us
    reduce_scatter x1, waiting for transfers between devices, shards(): lax.psum_scatter(jnp.einsum('ctn,cdn->td', grad_proj, qkv_low, preferred_...  54.8 us
    reduce_scatter x1, waiting for transfers between devices, shards(): lax.psum_scatter(jnp.einsum('ctf,cdf->td', grad_both, in_low, preferred_e...  53.5 us
    unnamed x135, local copies, waits for them, and re-layouts  38 us
    reduce_scatter x1, waiting for transfers between devices, shards(): lax.psum_scatter(jnp.dot(lax.slice_in_dim(hidden, 0, lax.axis_size('tenso...  37.2 us
    all_gather x1, blocking collectives, shards(): lax.all_gather(w_in.astype(jnp.bfloat16), 'dp', axis=1, tiled=True)  36.1 us
  transfers between devices with their start and end apart: 13, of which 8 were waited for; matrix products, arithmetic and copies ran while one was open for 25% of the time, Pallas kernels for 0%

commit v1 on v0

v1 whole, which is shorter than its diff:
```python
import functools

import jax
import jax.numpy as jnp
import numpy as np
from jax import lax
from jax.experimental import pallas as pl
from jax.experimental.pallas import tpu as pltpu
from jax.sharding import PartitionSpec as P

HD = 64
L = 1024
STEP = 10


eps_norm = 1e-05
rope_base = 160000.0
beta_one = 0.9
beta_two = 0.98
adam_eps = 1e-06
weight_rate = 0.02
gain_rate = 0.2
weight_decay = 0.01

low = jnp.bfloat16
full = jnp.float32
ROWS = 256
PAIR = 2 * HD
VMEM_BYTES = 52 << 20


def dot(left, right, left_dim, right_dim):
    return lax.dot_general(
        left, right, (((left_dim,), (right_dim,)), ((), ())), preferred_element_type=full
    )


def params():
    return pltpu.CompilerParams(vmem_limit_bytes=VMEM_BYTES)


def whole(shape):
    return pl.BlockSpec(shape, lambda *_: (0,) * len(shape))


def rows_of(width, index=lambda i: i):
    return pl.BlockSpec((ROWS, width), lambda i: (index(i), 0))


def own_half(i):
    return jnp.minimum(i, L // ROWS // 2 - 1)


def other_half(i):
    return jnp.maximum(i - L // ROWS // 2, 0)


def swapped(i):
    return (i + L // ROWS // 2) % (L // ROWS)


def is_own(i):
    return i < L // ROWS // 2


def core_swap(array):
    return lax.ppermute(array, "tensor", [(t, t ^ 1) for t in range(4)])


def y_swap(array):
    return lax.ppermute(array, "tensor", [(t, t ^ 2) for t in range(4)])


def x_swap(array, count):
    return lax.ppermute(array, "dp", [(d, d ^ 1) for d in range(count)])


def z_shift(array, count, step):
    around = count // 2
    return lax.ppermute(
        array, "dp", [(d, (d // 2 + step) % around * 2 + d % 2) for d in range(count)]
    )


def staged(count):
    return count == 8


def assemble_kernel(widths, place_ref, za, xa, ya, zb, yb, xb, *outs):
    place = place_ref[0]
    half = za.shape[1]
    for jx in range(2):
        for jz in range(4):
            source = (place // 2 + 4 - jz) % 4 * 2 + (place % 2 + jx) % 2
            own_a = (za, xa)[jx][jz]
            other_a = ya[jx, jz]
            own_b = zb[jz] if jx == 0 else xb[0, jz]
            other_b = yb[jz] if jx == 0 else xb[1, jz]
            for part, (own, other) in enumerate(((own_a, other_a), (own_b, other_b))):
                start = pl.multiple_of(source * 2 * half + part * half, half)
                offset = 0
                for width, out in zip(widths, outs):
                    out[pl.ds(start, half), :] = jnp.concatenate(
                        [own[:, offset : offset + width], other[:, offset : offset + width]], axis=1
                    )
                    offset += width


def gather_weights(parts, count):
    widths = [part.shape[1] for part in parts]
    shard = jnp.concatenate(parts, axis=1)
    height, total = shard.shape
    if not staged(count):
        own = lax.all_gather(shard, "dp", axis=0, tiled=True)
        other = y_swap(own)
        gathered, offset = [], 0
        for width in widths:
            gathered.append(
                jnp.concatenate(
                    [own[:, offset : offset + width], other[:, offset : offset + width]], axis=1
                )
            )
            offset += width
        return gathered
    half = height // 2
    along_z = [shard] + [z_shift(shard, count, step) for step in (1, 2, 3)]
    za = jnp.stack([piece[:half] for piece in along_z])
    zb = jnp.stack([piece[half:] for piece in along_z])
    xa = x_swap(za, count)
    yb = y_swap(zb)
    ya = y_swap(jnp.stack([za, xa]))
    xb = x_swap(jnp.stack([zb, yb]), count)
    place = lax.axis_index("dp").astype(jnp.int32)[None]
    return pl.pallas_call(
        functools.partial(assemble_kernel, widths),
        in_specs=[pl.BlockSpec(memory_space=pltpu.SMEM)]
        + [pl.BlockSpec(memory_space=pltpu.VMEM)] * 6,
        out_specs=[pl.BlockSpec(memory_space=pltpu.VMEM)] * len(widths),
        out_shape=[jax.ShapeDtypeStruct((height * count, 2 * width), low) for width in widths],
        compiler_params=params(),
        name="assemble",
    )(place, za, xa, ya, zb, yb, xb)


def weight_grad_kernel(pairs, sources, fast, place_ref, *refs):
    ins, outs, scratch = refs[: sources], refs[sources : sources + 4], refs[sources + 4 :]
    place = place_ref[0]
    for (left, right), held in zip(pairs, scratch):
        held[...] = dot(ins[left][...], ins[right][...], 0, 0)
    if not fast:
        offset = 0
        for held in scratch:
            width = held.shape[1] // 2
            outs[0][:, offset : offset + width] = held[:, :width].astype(low)
            outs[1][:, offset : offset + width] = held[:, width:].astype(low)
            offset += width
        return
    ay, by, ax, bx = outs
    half = ay.shape[2]
    for jx in range(2):
        for jz in range(4):
            target = (place // 2 + jz) % 4 * 2 + (place % 2 + jx) % 2
            for part in range(2):
                start = pl.multiple_of(target * 2 * half + part * half, half)
                own, other = [], []
                for held in scratch:
                    width = held.shape[1] // 2
                    rows = held[pl.ds(start, half), :].astype(low)
                    own.append(rows[:, :width])
                    other.append(rows[:, width:])
                own = jnp.concatenate(own, axis=1)
                other = jnp.concatenate(other, axis=1)
                if part == 0:
                    ay[jx, jz] = own
                    by[jx, jz] = other
                else:
                    (ax, bx)[jx][0, jz] = own
                    (ax, bx)[jx][1, jz] = other


def reduced_weight_grad(arrays, pairs, count):
    depth = arrays[pairs[0][0]].shape[1]
    widths = [arrays[right].shape[1] for _, right in pairs]
    total = sum(widths) // 2
    fast = staged(count)
    if fast:
        half = depth // count // 2
        outs = [jax.ShapeDtypeStruct((2, 4, half, total), low)] * 4
    else:
        outs = [jax.ShapeDtypeStruct((depth, total), low)] * 2 + [
            jax.ShapeDtypeStruct((8, 128), low)
        ] * 2
    place = lax.axis_index("dp").astype(jnp.int32)[None]
    flops = 2 * depth * sum(widths) * L
    first, second, third, fourth = pl.pallas_call(
        functools.partial(weight_grad_kernel, pairs, len(arrays), fast),
        in_specs=[pl.BlockSpec(memory_space=pltpu.SMEM)]
        + [pl.BlockSpec(memory_space=pltpu.VMEM)] * len(arrays),
        out_specs=[pl.BlockSpec(memory_space=pltpu.VMEM)] * 4,
        out_shape=outs,
        scratch_shapes=[pltpu.VMEM((depth, width), full) for width in widths],
        compiler_params=params(),
        cost_estimate=pl.CostEstimate(
            flops=flops, bytes_accessed=4 * depth * sum(widths), transcendentals=0
        ),
        name="weight_grad",
    )(place, *arrays)
    if not fast:
        summed = first.astype(full) + y_swap(second).astype(full)
        return lax.psum_scatter(summed, "dp", scatter_dimension=0, tiled=True)

    def add(here, there):
        return (here.astype(full) + there.astype(full)).astype(low)

    from_y = y_swap(second)
    from_x = x_swap(fourth, count)
    part_a = add(first, from_y)
    part_b = add(third, from_x)
    next_a = x_swap(part_a[1], count)
    next_b = y_swap(part_b[1])
    merged = jnp.concatenate([add(part_a[0], next_a), add(part_b[0], next_b)], axis=1)
    result = merged[0].astype(full)
    for step in (1, 2, 3):
        result = result + z_shift(merged[step], count, step).astype(full)
    return result


def sum_everywhere(array, count):
    array = array + core_swap(array)
    array = array + y_swap(array)
    if not staged(count):
        return lax.psum(array, "dp")
    array = array + x_swap(array, count)
    return array + sum(z_shift(array, count, step) for step in (1, 2, 3))


def gather_gains(gains, count):
    if not staged(count):
        return lax.all_gather(gains, "dp", axis=1, tiled=True)
    along_z = jnp.stack([gains] + [z_shift(gains, count, step) for step in (1, 2, 3)])
    pieces = jnp.concatenate([along_z, x_swap(along_z, count)])
    place = lax.axis_index("dp")
    order = np.arange(count)
    sources = (place // 2 + 4 - order % 4) % 4 * 2 + (place % 2 + order // 4) % 2
    chosen = sources[:, None] == order[None, :]
    spread = jnp.where(chosen[:, :, None, None], pieces[:, None], 0.0).sum(axis=0)
    return spread.transpose(1, 0, 2).reshape(gains.shape[0], -1)


def normalized(values):
    centred = values - jnp.mean(values, axis=-1, keepdims=True)
    spread = jnp.mean(centred * centred, axis=-1, keepdims=True)
    scale = lax.rsqrt(spread + eps_norm)
    return centred * scale, scale


def norm_back(values, scales, grads):
    unit, scale = normalized(values)
    inner = grads * scales
    mean_inner = jnp.mean(inner, axis=-1, keepdims=True)
    mean_unit = jnp.mean(inner * unit, axis=-1, keepdims=True)
    return scale * (inner - mean_inner - unit * mean_unit), jnp.sum(
        grads * unit, axis=0, keepdims=True
    )


def rope_tables(offset):
    half_width = HD // 2
    frequency = rope_base ** (-(jnp.arange(half_width, dtype=full) * 2.0 / HD))
    position = ((jnp.arange(L) + offset) % L).astype(full)
    angles = position[:, None] * frequency[None, :]
    cosine, sine = jnp.cos(angles), jnp.sin(angles)
    return (
        jnp.concatenate([cosine] * 4, axis=1),
        jnp.concatenate([-sine, sine, -sine, sine], axis=1),
    )


def turn(values, cosine, sine):
    lane = lax.broadcasted_iota(jnp.int32, values.shape, 1)
    ahead = pltpu.roll(values, PAIR - HD // 2, 1)
    behind = pltpu.roll(values, HD // 2, 1)
    turned = jnp.where(lane % HD < HD // 2, ahead, behind)
    return values * cosine + turned * sine


def qkv_kernel(x_own, x_other, gain, wq, wk, wv, cosine, sine, normed, q_out, k_out, v_out):
    values = jnp.where(is_own(pl.program_id(0)), x_own[...], x_other[...]).astype(full)
    unit, _ = normalized(values)
    rows = (unit * gain[...]).astype(low)
    normed[...] = rows
    query = dot(rows, wq[...], 1, 0)
    key = dot(rows, wk[...], 1, 0)
    for start in range(0, query.shape[1], PAIR):
        lanes = slice(start, start + PAIR)
        turned = turn(query[:, lanes], cosine[...], sine[...]).astype(low)
        q_out[:, lanes] = turned * jnp.asarray(HD ** (-0.5), low)
        k_out[:, lanes] = turn(key[:, lanes], cosine[...], sine[...]).astype(low)
    v_out[...] = dot(rows, wv[...], 1, 0).astype(low)


def project(x_own, x_other, gain, wq, wk, wv, cosine, sine):
    depth, width = wq.shape
    return pl.pallas_call(
        qkv_kernel,
        grid=(L // ROWS,),
        in_specs=[
            rows_of(depth, own_half),
            rows_of(depth, other_half),
            whole((1, depth)),
            whole((depth, width)),
            whole((depth, width)),
            whole((depth, width)),
            rows_of(PAIR),
            rows_of(PAIR),
        ],
        out_specs=[rows_of(depth), rows_of(width), rows_of(width), rows_of(width)],
        out_shape=[jax.ShapeDtypeStruct((L, depth), low)]
        + [jax.ShapeDtypeStruct((L, width), low)] * 3,
        compiler_params=params(),
        cost_estimate=pl.CostEstimate(
            flops=6 * L * depth * width, bytes_accessed=8 * L * depth, transcendentals=0
        ),
        name="project",
    )(x_own, x_other, gain, wq, wk, wv, cosine, sine)


def head_masks(height):
    lane = lax.broadcasted_iota(jnp.int32, (height, PAIR), 1)
    return [(lane // HD == head).astype(full).astype(low) for head in range(2)]


def attend_kernel(q_ref, k_ref, v_ref, mixed, lse_ref):
    keys, values = k_ref[...], v_ref[...]
    masks = head_masks(ROWS)
    lane = lax.broadcasted_iota(jnp.int32, (ROWS, PAIR), 1)
    for start in range(0, L, ROWS):
        rows = slice(start, start + ROWS)
        query = q_ref[rows, :]
        results = []
        for head in range(2):
            scores = dot(query * masks[head], keys, 1, 1)
            row_max = jnp.max(scores, axis=1, keepdims=True)
            raised = jnp.exp(scores - row_max)
            total = jnp.sum(raised, axis=1, keepdims=True)
            results.append(dot(raised.astype(low), values, 1, 0) / total)
            lse = jnp.broadcast_to(row_max + jnp.log(total), (ROWS, PAIR))
            lse_ref[0, head : head + 1, rows] = lse.T[0:1]
        mixed[rows, :] = jnp.where(lane < HD, results[0], results[1]).astype(low)


def attend(query, key, value):
    width = query.shape[1]
    pairs = width // PAIR
    block = pl.BlockSpec((L, PAIR), lambda i: (0, i))
    totals = pl.BlockSpec((1, 2, L), lambda i: (i, 0, 0))
    return pl.pallas_call(
        attend_kernel,
        grid=(pairs,),
        in_specs=[block] * 3,
        out_specs=[block, totals],
        out_shape=[
            jax.ShapeDtypeStruct((L, width), low),
            jax.ShapeDtypeStruct((pairs, 2, L), full),
        ],
        compiler_params=params(),
        cost_estimate=pl.CostEstimate(
            flops=16 * L * L * width, bytes_accessed=8 * L * width, transcendentals=2 * pairs * L * L
        ),
        name="attend",
    )(query, key, value)


def attend_back_kernel(
    q_ref, k_ref, v_ref, o_ref, grad_ref, lse_ref, cosine, sine, dq_out, dk_out, dv_out, dk, dv
):
    masks = head_masks(L)
    chunk_masks = head_masks(ROWS)
    keys, values = k_ref[...], v_ref[...]
    head_keys = [keys * mask for mask in masks]
    head_values = [values * mask for mask in masks]
    product = (grad_ref[...].astype(full) * o_ref[...].astype(full)).T
    inner = [jnp.sum(product[head * HD : (head + 1) * HD], axis=0, keepdims=True) for head in range(2)]
    for start in range(0, L, ROWS):
        rows = slice(start, start + ROWS)
        query, grad = q_ref[rows, :], grad_ref[rows, :]
        dq = None
        for head in range(2):
            scores = dot(head_keys[head], query, 1, 1)
            probs = jnp.exp(scores - lse_ref[0, head : head + 1, rows])
            grad_probs = dot(head_values[head], grad, 1, 1)
            grad_scores = (probs * (grad_probs - inner[head][:, rows])).astype(low)
            add_v = dot(probs.astype(low), grad * chunk_masks[head], 1, 0)
            add_k = dot(grad_scores, query * chunk_masks[head], 1, 0)
            add_q = dot(grad_scores, head_keys[head], 0, 0)
            dq = add_q if dq is None else dq + add_q
            if start == 0 and head == 0:
                dv[...] = add_v
                dk[...] = add_k
            else:
                dv[...] += add_v
                dk[...] += add_k
        dq_out[rows, :] = turn(dq * HD ** (-0.5), cosine[rows, :], -sine[rows, :]).astype(low)
    dk_out[...] = turn(dk[...], cosine[...], -sine[...]).astype(low)
    dv_out[...] = dv[...].astype(low)


def attend_back(query, key, value, mixed, grad, lse, cosine, sine):
    width = query.shape[1]
    pairs = width // PAIR
    block = pl.BlockSpec((L, PAIR), lambda i: (0, i))
    totals = pl.BlockSpec((1, 2, L), lambda i: (i, 0, 0))
    return pl.pallas_call(
        attend_back_kernel,
        grid=(pairs,),
        in_specs=[block] * 5 + [totals] + [whole((L, PAIR))] * 2,
        out_specs=[block] * 3,
        out_shape=[jax.ShapeDtypeStruct((L, width), low)] * 3,
        scratch_shapes=[pltpu.VMEM((L, PAIR), full)] * 2,
        compiler_params=params(),
        cost_estimate=pl.CostEstimate(
            flops=40 * L * L * width, bytes_accessed=16 * L * width, transcendentals=2 * pairs * L * L
        ),
        name="attend_back",
    )(query, key, value, mixed, grad, lse, cosine, sine)


def feed_forward_kernel(
    mixed_own,
    mixed_other,
    x_own,
    x_other,
    dy_own,
    dy_other,
    gain,
    wo_own,
    wo_other,
    w_gate,
    w_up,
    w_down,
    resid_out,
    normed,
    hidden_out,
    dgate_out,
    dup_out,
    out_own,
    out_other,
    dnormed,
    dnormed_low,
):
    step = pl.program_id(0)
    own = is_own(step)
    tokens = jnp.where(own, x_own[...], x_other[...]).astype(full)
    pull = jnp.where(own, dy_own[...], dy_other[...])
    resid = (
        tokens + dot(mixed_own[...], wo_own[...], 1, 1) + dot(mixed_other[...], wo_other[...], 1, 1)
    )
    resid_out[...] = resid
    unit, _ = normalized(resid)
    rows = (unit * gain[...]).astype(low)
    normed[...] = rows
    gate = dot(rows, w_gate[...], 1, 0)
    up = dot(rows, w_up[...], 1, 0)
    cumulative = 0.5 + 0.5 * lax.erf(gate * np.float32(0.5**0.5))
    density = jnp.exp(gate * gate * -0.5) * np.float32((2.0 * np.pi) ** -0.5)
    activated = gate * cumulative
    hidden = (activated * up).astype(low)
    hidden_out[...] = hidden
    part = dot(hidden, w_down[...], 1, 1)

    @pl.when(own)
    def _():
        out_own[...] = resid + part

    @pl.when(jnp.logical_not(own))
    def _():
        out_other[...] = part.astype(low)

    dhidden = dot(pull, w_down[...], 1, 0)
    dgate = (dhidden * up * (cumulative + gate * density)).astype(low)
    dup = (dhidden * activated).astype(low)
    dgate_out[...] = dgate
    dup_out[...] = dup
    grad = dot(dgate, w_gate[...], 1, 1) + dot(dup, w_up[...], 1, 1)
    dnormed[...] = grad
    dnormed_low[...] = grad.astype(low)


def feed_forward(
    mixed, mixed_other, x_own, x_other, dy_own, dy_other, gain, wo, wo_other, w_gate, w_up, w_down
):
    depth, width = wo.shape
    units = w_gate.shape[1]
    half = L // 2
    return pl.pallas_call(
        feed_forward_kernel,
        grid=(L // ROWS,),
        in_specs=[
            rows_of(width),
            rows_of(width, swapped),
            rows_of(depth, own_half),
            rows_of(depth, other_half),
            rows_of(depth, own_half),
            rows_of(depth, other_half),
            whole((1, depth)),
            whole((depth, width)),
            whole((depth, width)),
            whole((depth, units)),
            whole((depth, units)),
            whole((depth, units)),
        ],
        out_specs=[
            rows_of(depth),
            rows_of(depth),
            rows_of(units),
            rows_of(units),
            rows_of(units),
            rows_of(depth, own_half),
            rows_of(depth, other_half),
            rows_of(depth),
            rows_of(depth),
        ],
        out_shape=[
            jax.ShapeDtypeStruct((L, depth), full),
            jax.ShapeDtypeStruct((L, depth), low),
            jax.ShapeDtypeStruct((L, units), low),
            jax.ShapeDtypeStruct((L, units), low),
            jax.ShapeDtypeStruct((L, units), low),
            jax.ShapeDtypeStruct((half, depth), full),
            jax.ShapeDtypeStruct((half, depth), low),
            jax.ShapeDtypeStruct((L, depth), full),
            jax.ShapeDtypeStruct((L, depth), low),
        ],
        compiler_params=params(),
        cost_estimate=pl.CostEstimate(
            flops=2 * L * depth * (2 * width + 6 * units),
            bytes_accessed=24 * L * depth,
            transcendentals=2 * L * units,
        ),
        name="feed_forward",
    )(mixed, mixed_other, x_own, x_other, dy_own, dy_other, gain, wo, wo_other, w_gate, w_up, w_down)


def resid_back_kernel(
    resid, grad_own, grad_other, dy_own, dy_other, gain, wo, dresid, dresid_low, dmixed, gain_grad
):
    step = pl.program_id(0)
    own = is_own(step)
    pull = jnp.where(own, dy_own[...], dy_other[...]).astype(full)
    grads = grad_own[...] + grad_other[...].astype(full)
    back, gain_part = norm_back(resid[...], gain[...], grads)
    total = pull + back
    rounded = total.astype(low)
    dresid_low[...] = rounded
    dmixed[...] = dot(rounded, wo[...], 1, 0).astype(low)

    @pl.when(step == 0)
    def _():
        gain_grad[...] = jnp.zeros_like(gain_grad)

    @pl.when(own)
    def _():
        dresid[...] = total
        gain_grad[...] += gain_part


def resid_back(resid, grad_own, grad_other, dy_own, dy_other, gain, wo):
    depth, width = wo.shape
    return pl.pallas_call(
        resid_back_kernel,
        grid=(L // ROWS,),
        in_specs=[
            rows_of(depth),
            rows_of(depth),
            rows_of(depth, swapped),
            rows_of(depth, own_half),
            rows_of(depth, other_half),
            whole((1, depth)),
            whole((depth, width)),
        ],
        out_specs=[rows_of(depth, own_half), rows_of(depth), rows_of(width), whole((1, depth))],
        out_shape=[
            jax.ShapeDtypeStruct((L // 2, depth), full),
            jax.ShapeDtypeStruct((L, depth), low),
            jax.ShapeDtypeStruct((L, width), low),
            jax.ShapeDtypeStruct((1, depth), full),
        ],
        compiler_params=params(),
        cost_estimate=pl.CostEstimate(
            flops=2 * L * depth * width, bytes_accessed=16 * L * depth, transcendentals=0
        ),
        name="resid_back",
    )(resid, grad_own, grad_other, dy_own, dy_other, gain, wo)


def project_back_kernel(dq, dk, dv, wq, wk, wv, grad_own, grad_other):
    grad = (
        dot(dq[...], wq[...], 1, 1) + dot(dk[...], wk[...], 1, 1) + dot(dv[...], wv[...], 1, 1)
    )
    own = is_own(pl.program_id(0))

    @pl.when(own)
    def _():
        grad_own[...] = grad

    @pl.when(jnp.logical_not(own))
    def _():
        grad_other[...] = grad.astype(low)


def project_back(dq, dk, dv, wq, wk, wv):
    depth, width = wq.shape
    return pl.pallas_call(
        project_back_kernel,
        grid=(L // ROWS,),
        in_specs=[rows_of(width)] * 3 + [whole((depth, width))] * 3,
        out_specs=[rows_of(depth, own_half), rows_of(depth, other_half)],
        out_shape=[
            jax.ShapeDtypeStruct((L // 2, depth), full),
            jax.ShapeDtypeStruct((L // 2, depth), low),
        ],
        compiler_params=params(),
        cost_estimate=pl.CostEstimate(
            flops=6 * L * depth * width, bytes_accessed=8 * L * depth, transcendentals=0
        ),
        name="project_back",
    )(dq, dk, dv, wq, wk, wv)


def input_back_kernel(tokens, grad_own, grad_other, dresid, gain, result, gain_grad):
    grads = grad_own[...] + grad_other[...].astype(full)
    back, gain_part = norm_back(tokens[...].astype(full), gain[...], grads)
    result[...] = dresid[...] + back

    @pl.when(pl.program_id(0) == 0)
    def _():
        gain_grad[...] = jnp.zeros_like(gain_grad)

    gain_grad[...] += gain_part


def input_back(tokens, grad_own, grad_other, dresid, gain):
    height, depth = tokens.shape
    return pl.pallas_call(
        input_back_kernel,
        grid=(height // ROWS,),
        in_specs=[rows_of(depth)] * 4 + [whole((1, depth))],
        out_specs=[rows_of(depth), whole((1, depth))],
        out_shape=[
            jax.ShapeDtypeStruct((height, depth), full),
            jax.ShapeDtypeStruct((1, depth), full),
        ],
        compiler_params=params(),
        cost_estimate=pl.CostEstimate(
            flops=20 * height * depth, bytes_accessed=16 * height * depth, transcendentals=0
        ),
        name="input_back",
    )(tokens, grad_own, grad_other, dresid, gain)


def adamw(weight, grad, first, second, rate, decay):
    first_new = beta_one * first + (1.0 - beta_one) * grad
    second_new = beta_two * second + (1.0 - beta_two) * grad * grad
    step_size = (
        first_new
        / (1.0 - beta_one**STEP)
        / (jnp.sqrt(second_new / (1.0 - beta_two**STEP)) + adam_eps)
    )
    return (weight - rate * (step_size + decay * weight), first_new, second_new)


def shards(
    tokens,
    cotangent,
    w_qkv,
    w_attn_out,
    w_in,
    w_mlp_out,
    gains,
    first_qkv,
    first_attn_out,
    first_in,
    first_mlp_out,
    first_gains,
    second_qkv,
    second_attn_out,
    second_in,
    second_mlp_out,
    second_gains,
):
    count = lax.axis_size("dp")
    core = lax.axis_index("tensor") % 2
    place = lax.axis_index("dp")
    x_other = core_swap(tokens)
    gains_all = gather_gains(gains, count)
    gain_one, gain_two = gains_all[0:1], gains_all[1:2]
    wq, wk, wv = gather_weights([w_qkv[c].astype(low) for c in range(3)], count)
    wo, w_gate, w_up, w_down = gather_weights(
        [w_attn_out.astype(low).T, w_in[0].astype(low), w_in[1].astype(low), w_mlp_out.astype(low).T],
        count,
    )
    wo_other = core_swap(wo)
    dy_other = core_swap(cotangent)
    cosine, sine = rope_tables(core * (L // 2))

    normed_one, query, key, value = project(
        tokens, x_other, gain_one, wq, wk, wv, cosine, sine
    )
    mixed, lse = attend(query, key, value)
    mixed_other = core_swap(mixed)
    resid, normed_two, hidden, dgate, dup, out_own, out_other, dnormed, dnormed_low = feed_forward(
        mixed,
        mixed_other,
        tokens,
        x_other,
        cotangent,
        dy_other,
        gain_two,
        wo,
        wo_other,
        w_gate,
        w_up,
        w_down,
    )
    dnormed_other = core_swap(dnormed_low)
    output = (out_own + core_swap(out_other).astype(full)).astype(low)
    dy_rows = jnp.concatenate([cotangent, dy_other])
    grad_mlp = reduced_weight_grad(
        [normed_two, dgate, dup, dy_rows, hidden], [(0, 1), (0, 2), (3, 4)], count
    )
    dresid, dresid_low, dmixed, grad_gain_two = resid_back(
        resid, dnormed, dnormed_other, cotangent, dy_other, gain_two, wo
    )
    dq, dk, dv = attend_back(query, key, value, mixed, dmixed, lse, cosine, sine)
    grad_attn = reduced_weight_grad([dresid_low, mixed], [(0, 1)], count)
    grad_proj = reduced_weight_grad([normed_one, dq, dk, dv], [(0, 1), (0, 2), (0, 3)], count)
    grad_one, grad_one_low = project_back(dq, dk, dv, wq, wk, wv)
    grad_inputs, grad_gain_one = input_back(
        tokens, grad_one, core_swap(grad_one_low), dresid, gain_one
    )
    grad_gains = sum_everywhere(jnp.concatenate([grad_gain_one, grad_gain_two]), count)

    head_width = w_qkv.shape[2]
    unit_width = w_in.shape[2]
    shard_qkv = jnp.stack([grad_proj[:, c * head_width : (c + 1) * head_width] for c in range(3)])
    shard_attn = grad_attn.T
    shard_in = jnp.stack([grad_mlp[:, c * unit_width : (c + 1) * unit_width] for c in range(2)])
    shard_down = grad_mlp[:, 2 * unit_width :].T
    shard_gain = lax.dynamic_slice_in_dim(grad_gains, place * gains.shape[1], gains.shape[1], axis=1)

    new_qkv = adamw(w_qkv, shard_qkv, first_qkv, second_qkv, weight_rate, weight_decay)
    new_attn = adamw(
        w_attn_out, shard_attn, first_attn_out, second_attn_out, weight_rate, weight_decay
    )
    new_in = adamw(w_in, shard_in, first_in, second_in, weight_rate, weight_decay)
    new_down = adamw(
        w_mlp_out, shard_down, first_mlp_out, second_mlp_out, weight_rate, weight_decay
    )
    new_gain = adamw(gains, shard_gain, first_gains, second_gains, gain_rate, 0.0)
    return (
        output,
        grad_inputs,
        shard_qkv,
        shard_attn,
        shard_in,
        shard_down,
        shard_gain,
        new_qkv[0],
        new_attn[0],
        new_in[0],
        new_down[0],
        new_gain[0],
        new_qkv[1],
        new_attn[1],
        new_in[1],
        new_down[1],
        new_gain[1],
        new_qkv[2],
        new_attn[2],
        new_in[2],
        new_down[2],
        new_gain[2],
    )


def solution(mesh):
    return jax.shard_map(
        shards,
        mesh=mesh,
        in_specs=(
            P(("dp", "tensor"), None),
            P(("dp", "tensor"), None),
            P(None, "dp", "tensor"),
            P("tensor", "dp"),
            P(None, "dp", "tensor"),
            P("tensor", "dp"),
            P(None, "dp"),
            P(None, "dp", "tensor"),
            P("tensor", "dp"),
            P(None, "dp", "tensor"),
            P("tensor", "dp"),
            P(None, "dp"),
            P(None, "dp", "tensor"),
            P("tensor", "dp"),
            P(None, "dp", "tensor"),
            P("tensor", "dp"),
            P(None, "dp"),
        ),
        out_specs=(
            P(("dp", "tensor"), None),
            P(("dp", "tensor"), None),
            P(None, "dp", "tensor"),
            P("tensor", "dp"),
            P(None, "dp", "tensor"),
            P("tensor", "dp"),
            P(None, "dp"),
            P(None, "dp", "tensor"),
            P("tensor", "dp"),
            P(None, "dp", "tensor"),
            P("tensor", "dp"),
            P(None, "dp"),
            P(None, "dp", "tensor"),
            P("tensor", "dp"),
            P(None, "dp", "tensor"),
            P("tensor", "dp"),
            P(None, "dp"),
            P(None, "dp", "tensor"),
            P("tensor", "dp"),
            P(None, "dp", "tensor"),
            P("tensor", "dp"),
            P(None, "dp"),
        ),
        check_vma=False,
    )
```

time: 888 us -> 308 us (0.35); the launches traced: 873 us -> 304 us
  waiting for transfers between devices: 373 us -> 90.3 us
  blocking collectives: 165 us -> 0 us
  local copies, waits for them, and re-layouts: 136 us -> 23 us
  matrix products: 111 us -> 0 us
  Pallas kernels: 0 us -> 97.7 us
  starting transfers between devices: 1.19 us -> 69 us
  other arithmetic: 70.4 us -> 22.2 us
  between operations: 15.2 us -> 1.65 us
    reduce_scatter x4 -> x0, waiting for transfers between devices: 203 us -> none  [the longest x1 57.7 us: shards(): lax.psum_scatter(jnp.dot(lax.slice_in_dim(mixed, 0, rows_local * lax.axis...]
    unnamed x18 -> x0, waiting for transfers between devices: 164 us -> none
    all_gather x5 -> x0, blocking collectives: 159 us -> none  [the longest x1 36.1 us: shards(): lax.all_gather(w_in.astype(jnp.bfloat16), 'dp', axis=1, tiled=True)]
    dot_general x37 -> x0, matrix products: 98 us -> none  [the longest x4 11.6 us: attend_backward(): jnp.einsum('qhd,khd->hqk', grad_part, values, preferred_element_type=jnp....]
    pallas_call x0 -> x12, Pallas kernels: none -> 97.7 us  [the longest x1 19.6 us: attend_back(): pl.pallas_call(attend_back_kernel, grid=(pairs,), in_specs=[block] * 5 +...]
    ppermute x0 -> x52, waiting for transfers between devices: none -> 90.3 us  [the longest x12 50.2 us: x_swap(): return lax.ppermute(array, 'dp', [(d, d ^ 1) for d in range(count)])]
    ppermute x0 -> x52, starting transfers between devices: none -> 69 us  [the longest x21 38.2 us: z_shift(): lax.ppermute(array, 'dp', [(d, (d // 2 + step) % around * 2 + d % 2) for...]
    dynamic_update_slice x8 -> x0, local copies, waits for them, and re-layouts: 60.5 us -> none  [shards(): attended, totals = lax.map(attend_forward, (queries, keys, values))]
  transfers between devices with their start and end apart: 13 -> 52, of which waited for: 8 -> 19; matrix products, arithmetic and copies ran while one was open for 25% -> 12% of each run, Pallas kernels for 0% -> 19%
where the time goes in v1:
time: 308 us; the launch traced here: 304 us
  Pallas kernels  97.7 us (32%)
  waiting for transfers between devices  90.3 us (29%)
  starting transfers between devices  69 us (22%)
  local copies, waits for them, and re-layouts  23 us (7%)
  other arithmetic  22.2 us (7%)
    ppermute x12, waiting for transfers between devices, x_swap(): return lax.ppermute(array, 'dp', [(d, d ^ 1) for d in range(count)])  50.2 us
    ppermute x21, starting transfers between devices, z_shift(): lax.ppermute(array, 'dp', [(d, (d // 2 + step) % around * 2 + d % 2) for...  38.2 us
    ppermute x21, waiting for transfers between devices, z_shift(): lax.ppermute(array, 'dp', [(d, (d // 2 + step) % around * 2 + d % 2) for...  23.7 us
    unnamed x76, local copies, waits for them, and re-layouts  19.8 us
    pallas_call x1, Pallas kernels, attend_back(): pl.pallas_call(attend_back_kernel, grid=(pairs,), in_specs=[block] * 5 +...  19.6 us
    pallas_call x1, Pallas kernels, feed_forward(): pl.pallas_call(feed_forward_kernel, grid=(L // ROWS,), in_specs=[rows_of(...  18.1 us
    ppermute x11, waiting for transfers between devices, y_swap(): return lax.ppermute(array, 'tensor', [(t, t ^ 2) for t in range(4)])  16.4 us
    pallas_call x3, Pallas kernels, reduced_weight_grad(): pl.pallas_call(functools.partial(weight_grad_kernel, pairs, len(arrays),...  15.9 us
  transfers between devices with their start and end apart: 52, of which 19 were waited for; matrix products, arithmetic and copies ran while one was open for 12% of the time, Pallas kernels for 19%

profile of v1, /device:TPU:0, one launch (start us, length us, event | category | flops | bytes accessed | tf_op | source)
XLA Modules:
  0.0 303.7 jit_solution(5411843354014157772)
XLA Ops:
  0.7 3.1 %collective-permute-start.1 = (f32[2,96]{1,0:T(2,128)}, f32[2,96]{1,0:T(2,128)S(1)}, u32[]{:S(2)}, u32[]{:S(2)}) collective-permute-start(f32[2,96]{1,0:T(2,128)} %param.26), channel_id=1, source_target_pairs={{0,8},{4,12},{8,16},{12,20},{16,24},{20,28},{24,0},{28,4},{1,9},{5... | collective-permute-start | bytes 2312 | tf_op jit(solution)/shard_map/ppermute | solution.py:80
  3.8 2.6 collective-permute-start.2
  15.7 2.9 collective-permute-start.7
  24.4 3.5 %collective-permute-start.16 = (bf16[96,1056]{1,0:T(8,128)(2,1)S(1)}, bf16[96,1056]{1,0:T(8,128)(2,1)S(1)}, u32[]{:S(2)}, u32[]{:S(2)}) collective-permute-start(bf16[96,1056]{1,0:T(8,128)(2,1)S(1)} %concatenate.35), channel_id=1, source_target_pairs={{0,24},{4,28},{8,0},{12,4},{16,8},{20,12},{24,16},{28,20},{1,25},{... | collective-permute-start | bytes 608264 | tf_op jit(solution)/shard_map/ppermute | solution.py:80
  31.2 6.7 %collective-permute-done.15 = bf16[96,1056]{1,0:T(8,128)(2,1)S(1)} collective-permute-done((bf16[96,1056]{1,0:T(8,128)(2,1)S(1)}, bf16[96,1056]{1,0:T(8,128)(2,1)S(1)}, u32[]{:S(2)}, u32[]{:S(2)}) %collective-permute-start.15) | collective-permute-done | bytes 202784 | tf_op jit(solution)/shard_map/ppermute | solution.py:80
  41.9 4.9 %collective-permute-done.8.xa = bf16[4,48,576]{2,1,0:T(8,128)(2,1)S(1)} collective-permute-done((bf16[4,48,576]{2,1,0:T(8,128)(2,1)S(1)}, bf16[4,48,576]{2,1,0:T(8,128)(2,1)S(1)}, u32[]{:S(2)}, u32[]{:S(2)}) %collective-permute-start.8) | collective-permute-done | bytes 221216 | tf_op jit(solution)/shard_map/ppermute | solution.py:75
  48.4 7.9 %collective-permute-done.17.xa = bf16[4,48,1056]{2,1,0:T(8,128)(2,1)S(1)} collective-permute-done((bf16[4,48,1056]{2,1,0:T(8,128)(2,1)S(1)}, bf16[4,48,1056]{2,1,0:T(8,128)(2,1)S(1)}, u32[]{:S(2)}, u32[]{:S(2)}) %collective-permute-start.17) | collective-permute-done | bytes 405536 | tf_op jit(solution)/shard_map/ppermute | solution.py:75
  58.6 6.0 %collective-permute-done.11.xb = bf16[2,4,48,576]{3,2,1,0:T(8,128)(2,1)S(1)} collective-permute-done((bf16[2,4,48,576]{3,2,1,0:T(8,128)(2,1)S(1)}, bf16[2,4,48,576]{3,2,1,0:T(8,128)(2,1)S(1)}, u32[]{:S(2)}, u32[]{:S(2)}) %collective-permute-start.11) | collective-permute-done | bytes 442400 | tf_op jit(solution)/shard_map/ppermute | solution.py:75
  66.1 4.4 %collective-permute-done.9.ya = bf16[2,4,48,576]{3,2,1,0:T(8,128)(2,1)S(1)} collective-permute-done((bf16[2,4,48,576]{3,2,1,0:T(8,128)(2,1)S(1)}, bf16[2,4,48,576]{3,2,1,0:T(8,128)(2,1)S(1)}, u32[]{:S(2)}, u32[]{:S(2)}) %collective-permute-start.9) | collective-permute-done | bytes 442400 | tf_op jit(solution)/shard_map/ppermute | solution.py:71
  73.1 6.9 %project.1 = (bf16[1024,768]{1,0:T(8,128)(2,1)}, bf16[1024,384]{1,0:T(8,128)(2,1)}, bf16[1024,384]{1,0:T(8,128)(2,1)}, bf16[1024,384]{1,0:T(8,128)(2,1)}) custom-call(bf16[512,768]{1,0:T(8,128)(2,1)} %tokens.1, bf16[512,768]{1,0:T(8,128)(2,1)} %collective-permute-done.x_other, f32[1,768]{1,0:T(1,128)S(1)} %slice.171.gain, bf16[768,384]{1,0:T(8,128)(2,1)S(1)} %copy-done.6, ...), custom_call_target="tpu_custom_call" | custom-call | flops 1811939328 | bytes 6291456 | tf_op jit(solution)/shard_map/project/pallas_call | solution.py:304
  81.1 13.8 %attend.1 = (bf16[1024,384]{1,0:T(8,128)(2,1)S(1)}, f32[3,2,1024]{2,1,0:T(2,128)S(1)}) custom-call(bf16[1024,384]{1,0:T(8,128)(2,1)S(1)} %copy-done.10, bf16[1024,384]{1,0:T(8,128)(2,1)} %get-tuple-element.71.k_ref, bf16[1024,384]{1,0:T(8,128)(2,1)} %get-tuple-element.72.v_ref), custom_call_target="tpu_custom_call" | custom-call | flops 6442450944 | bytes 3145728 | tf_op jit(solution)/shard_map/attend/pallas_call | solution.py:357
  97.0 4.1 %assemble.3 = (bf16[768,384]{1,0:T(8,128)(2,1)}, bf16[768,576]{1,0:T(8,128)(2,1)}, bf16[768,576]{1,0:T(8,128)(2,1)}, bf16[768,576]{1,0:T(8,128)(2,1)}) custom-call(s32[1]{0:T(128)} %bitcast.5.place_ref, bf16[4,48,1056]{2,1,0:T(8,128)(2,1)S(1)} %get-tuple-element.206.za, bf16[4,48,1056]{2,1,0:T(8,128)(2,1)S(1)} %collective-permute-done.17.xa, ...), custom_call_target="tpu_custom_call" | custom-call | tf_op jit(solution)/shard_map/assemble/pallas_call | solution.py:134
  101.5 2.7 pad_maximum_fusion.refs_3_
  104.3 18.1 %feed_forward.1 = (f32[1024,768]{1,0:T(8,128)}, bf16[1024,768]{1,0:T(8,128)(2,1)}, bf16[1024,576]{1,0:T(8,128)(2,1)}, bf16[1024,576]{1,0:T(8,128)(2,1)}, bf16[10...) custom-call(bf16[1024,384]{1,0:T(8,128)(2,1)} %copy-done.2, ...), custom_call_target="tpu_custom_call" | custom-call | flops 6643777536 | bytes 18874368 | tf_op jit(solution)/shard_map/feed_forward/pallas_call | solution.py:495
  122.4 8.4 %weight_grad.5 = (bf16[2,4,48,864]{3,2,1,0:T(8,128)(2,1)S(1)}, bf16[2,4,48,864]{3,2,1,0:T(8,128)(2,1)S(1)}, bf16[2,4,48,864]{3,2,1,0:T(8,128)(2,1)}, bf16[2,4,48,864]{3,2,1,0:T(8,128)(2,1)}) custom-call(s32[1]{0:T(128)} %bitcast.5.place_ref, bf16[1024,768]{1,0:T(8,128)(2,1)} %get-tuple-element.102.refs_0_, bf16[1024,576]{1,0:T(8,128)(2,1)} %get-tuple-element.103.refs_1_, ...), custom_call_target="tpu_custom_call" | custom-call | flops 2717908992 | bytes 5308416 | tf_op jit(solution)/shard_map/weight_grad/pallas_call | solution.py:195
  133.8 14.7 %collective-permute-done.41 = bf16[2,4,48,864]{3,2,1,0:T(8,128)(2,1)S(1)} collective-permute-done((bf16[2,4,48,864]{3,2,1,0:T(8,128)(2,1)}, bf16[2,4,48,864]{3,2,1,0:T(8,128)(2,1)S(1)}, u32[]{:S(2)}, u32[]{:S(2)}) %collective-permute-start.41) | collective-permute-done | bytes 663584 | tf_op jit(solution)/shard_map/ppermute | solution.py:75
  166.5 3.9 %collective-permute-start.44 = (bf16[96,864]{1,0:T(8,128)(2,1)S(1)}, bf16[96,864]{1,0:T(8,128)(2,1)S(1)}, u32[]{:S(2)}, u32[]{:S(2)}) collective-permute-start(bf16[96,864]{1,0:T(8,128)(2,1)S(1)} %get-tuple-element.199), channel_id=1, source_target_pairs={{0,16},{4,20},{8,24},{12,28},{16,0},{20,4},{24,8},{28,12},{1,17},{... | collective-permute-start | bytes 497672 | tf_op jit(solution)/shard_map/ppermute | solution.py:80
  172.6 2.5 collective-permute-done.43
  175.1 6.4 %collective-permute-done.44 = bf16[96,864]{1,0:T(8,128)(2,1)S(1)} collective-permute-done((bf16[96,864]{1,0:T(8,128)(2,1)S(1)}, bf16[96,864]{1,0:T(8,128)(2,1)S(1)}, u32[]{:S(2)}, u32[]{:S(2)}) %collective-permute-start.44) | collective-permute-done | bytes 165920 | tf_op jit(solution)/shard_map/ppermute | solution.py:80
  187.1 7.8 %resid_back.1 = (f32[512,768]{1,0:T(8,128)}, bf16[1024,768]{1,0:T(8,128)(2,1)}, bf16[1024,384]{1,0:T(8,128)(2,1)S(1)}, f32[1,768]{1,0:T(1,128)S(1)}) custom-call(f32[1024,768]{1,0:T(8,128)} %get-tuple-element.80.resid, f32[1024,768]{1,0:T(8,128)} %get-tuple-element.81.grad_own, bf16[1024,768]{1,0:T(8,128)(2,1)} %collective-permute-done.23.grad_other, ...), custom_call_target="tpu_custom_call" | custom-call | flops 603979776 | bytes 12582912 | tf_op jit(solution)/shard_map/resid_back/pallas_call | solution.py:569
  195.8 2.6 weight_grad.4
  199.6 19.6 %attend_back.1 = (bf16[1024,384]{1,0:T(8,128)(2,1)S(1)}, bf16[1024,384]{1,0:T(8,128)(2,1)}, bf16[1024,384]{1,0:T(8,128)(2,1)}) custom-call(bf16[1024,384]{1,0:T(8,128)(2,1)} %get-tuple-element.70.q_ref, bf16[1024,384]{1,0:T(8,128)(2,1)} %get-tuple-element.71.k_ref, bf16[1024,384]{1,0:T(8,128)(2,1)} %get-tuple-element.72.v_ref, bf16[1024,384]{1,0:T(8,128)(2,1)} %copy-done.2, ...), custom_call_target="tpu_custom_call" | custom-call | flops 16106127360 | bytes 6291456 | tf_op jit(solution)/shard_map/attend_back/pallas_call | solution.py:413
  220.1 5.0 %weight_grad.3 = (bf16[2,4,48,576]{3,2,1,0:T(8,128)(2,1)S(1)}, bf16[2,4,48,576]{3,2,1,0:T(8,128)(2,1)S(1)}, bf16[2,4,48,576]{3,2,1,0:T(8,128)(2,1)S(1)}, bf16[2,4,48,576]{3,2,1,0:T(8,128)(2,1)S(1)}) custom-call(s32[1]{0:T(128)} %bitcast.5.place_ref, bf16[1024,768]{1,0:T(8,128)(2,1)} %get-tuple-element.92.refs_0_, bf16[1024,384]{1,0:T(8,128)(2,1)} %copy-done.11, ...), custom_call_target="tpu_custom_call" | custom-call | flops 1811939328 | bytes 3538944 | tf_op jit(solution)/shard_map/weight_grad/pallas_call | solution.py:195
  231.4 8.3 %collective-permute-done.33 = bf16[4,48,192]{2,1,0:T(8,128)(2,1)S(1)} collective-permute-done((bf16[4,48,192]{2,1,0:T(8,128)(2,1)S(1)}, bf16[4,48,192]{2,1,0:T(8,128)(2,1)S(1)}, u32[]{:S(2)}, u32[]{:S(2)}) %collective-permute-start.33) | collective-permute-done | bytes 73760 | tf_op jit(solution)/shard_map/ppermute | solution.py:75
  239.8 4.3 %collective-permute-start.36 = (bf16[96,192]{1,0:T(8,128)(2,1)S(1)}, bf16[96,192]{1,0:T(8,128)(2,1)S(1)}, u32[]{:S(2)}, u32[]{:S(2)}) collective-permute-start(bf16[96,192]{1,0:T(8,128)(2,1)S(1)} %get-tuple-element.225), channel_id=1, source_target_pairs={{0,8},{4,12},{8,16},{12,20},{16,24},{20,28},{24,0},{28,4},{1,9},{5... | collective-permute-start | bytes 110600 | tf_op jit(solution)/shard_map/ppermute | solution.py:80
  246.5 6.3 %project_back.1 = (f32[512,768]{1,0:T(8,128)}, bf16[512,768]{1,0:T(8,128)(2,1)}) custom-call(bf16[1024,384]{1,0:T(8,128)(2,1)} %copy-done.11, bf16[1024,384]{1,0:T(8,128)(2,1)} %get-tuple-element.86.dk.refs_2_, bf16[1024,384]{1,0:T(8,128)(2,1)} %get-tuple-element.87.dv.refs_3_, bf16[768,384]{1,0:T(8,128)(2,1)S(1)} %copy-done.7, ...), custom_call_target="tpu_custom_call" | custom-call | flops 1811939328 | bytes 6291456 | tf_op jit(solution)/shard_map/project_back/pallas_call | solution.py:613
  259.3 7.7 %collective-permute-done.25 = bf16[2,4,48,576]{3,2,1,0:T(8,128)(2,1)} collective-permute-done((bf16[2,4,48,576]{3,2,1,0:T(8,128)(2,1)S(1)}, bf16[2,4,48,576]{3,2,1,0:T(8,128)(2,1)}, u32[]{:S(2)}, u32[]{:S(2)}) %collective-permute-start.25) | collective-permute-done | bytes 442400 | tf_op jit(solution)/shard_map/ppermute | solution.py:71
  271.8 3.6 %collective-permute-done.26 = bf16[4,48,576]{2,1,0:T(8,128)(2,1)S(1)} collective-permute-done((bf16[4,48,576]{2,1,0:T(8,128)(2,1)S(1)}, bf16[4,48,576]{2,1,0:T(8,128)(2,1)S(1)}, u32[]{:S(2)}, u32[]{:S(2)}) %collective-permute-start.26) | collective-permute-done | bytes 221216 | tf_op jit(solution)/shard_map/ppermute | solution.py:75
  275.5 3.5 %input_back.1 = (f32[512,768]{1,0:T(8,128)}, f32[1,768]{1,0:T(1,128)S(1)}) custom-call(bf16[512,768]{1,0:T(8,128)(2,1)S(1)} %copy-done.1, f32[512,768]{1,0:T(8,128)} %get-tuple-element.88.grad_own, bf16[512,768]{1,0:T(8,128)(2,1)S(1)} %collective-permute-done.24.grad_other, f32[512,768]{1,0:T(8,128)} %get-tuple-element.90.dresid, f32[1,768]{1,0:T(1,128)S(1)} %slice.171.gain), custom_call_target="tpu_custom_call" | custom-call | flops 7864320 | bytes 6291456 | tf_op jit(solution)/shard_map/input_back/pallas_call | solution.py:644
  284.7 2.6 collective-permute-done.29
  287.3 4.3 %collective-permute-done.30 = bf16[96,576]{1,0:T(8,128)(2,1)S(1)} collective-permute-done((bf16[96,576]{1,0:T(8,128)(2,1)S(1)}, bf16[96,576]{1,0:T(8,128)(2,1)S(1)}, u32[]{:S(2)}, u32[]{:S(2)}) %collective-permute-start.30) | collective-permute-done | bytes 110624 | tf_op jit(solution)/shard_map/ppermute | solution.py:80
  295.5 2.8 collective-permute-start.49
  (232 shorter events, 100.2 us)
Async XLA Ops:
  0.7 15.0 %collective-permute-start.1 = (f32[2,96]{1,0:T(2,128)}, f32[2,96]{1,0:T(2,128)S(1)}, u32[]{:S(2)}, u32[]{:S(2)}) collective-permute-start(f32[2,96]{1,0:T(2,128)} %param.26), channel_id=1, source_target_pairs={{0,8},{4,12},{8,16},{12,20},{16,24},{20,28},{24,0},{28,4},{1,9},{5... | collective-permute-start | bytes 2312 | tf_op jit(solution)/shard_map/ppermute | solution.py:80
  3.8 14.8 %collective-permute-start.2 = (f32[2,96]{1,0:T(2,128)}, f32[2,96]{1,0:T(2,128)S(1)}, u32[]{:S(2)}, u32[]{:S(2)}) collective-permute-start(f32[2,96]{1,0:T(2,128)} %param.26), channel_id=1, source_target_pairs={{0,16},{4,20},{8,24},{12,28},{16,0},{20,4},{24,8},{28,12},{1,17},{... | collective-permute-start | bytes 2312 | tf_op jit(solution)/shard_map/ppermute | solution.py:80
  6.3 12.8 %collective-permute-start.3 = (f32[2,96]{1,0:T(2,128)}, f32[2,96]{1,0:T(2,128)S(1)}, u32[]{:S(2)}, u32[]{:S(2)}) collective-permute-start(f32[2,96]{1,0:T(2,128)} %param.26), channel_id=1, source_target_pairs={{0,24},{4,28},{8,0},{12,4},{16,8},{20,12},{24,16},{28,20},{1,25},{... | collective-permute-start | bytes 2312 | tf_op jit(solution)/shard_map/ppermute | solution.py:80
  8.8 15.7 %collective-permute-start.5 = (bf16[96,576]{1,0:T(8,128)(2,1)S(1)}, bf16[96,576]{1,0:T(8,128)(2,1)S(1)}, u32[]{:S(2)}, u32[]{:S(2)}) collective-permute-start(bf16[96,576]{1,0:T(8,128)(2,1)S(1)} %pad_maximum_fusion.15), channel_id=1, source_target_pairs={{0,8},{4,12},{8,16},{12,20},{16,24},{20,28},{24,0},{28,4},{1,9},{5... | collective-permute-start | bytes 331784 | tf_op jit(solution)/shard_map/ppermute | solution.py:80
  9.5 18.4 %collective-permute-start.6 = (bf16[96,576]{1,0:T(8,128)(2,1)S(1)}, bf16[96,576]{1,0:T(8,128)(2,1)S(1)}, u32[]{:S(2)}, u32[]{:S(2)}) collective-permute-start(bf16[96,576]{1,0:T(8,128)(2,1)S(1)} %pad_maximum_fusion.15), channel_id=1, source_target_pairs={{0,16},{4,20},{8,24},{12,28},{16,0},{20,4},{24,8},{28,12},{1,17},{... | collective-permute-start | bytes 331784 | tf_op jit(solution)/shard_map/ppermute | solution.py:80
  15.7 12.4 %collective-permute-start.7 = (bf16[96,576]{1,0:T(8,128)(2,1)S(1)}, bf16[96,576]{1,0:T(8,128)(2,1)}, u32[]{:S(2)}, u32[]{:S(2)}) collective-permute-start(bf16[96,576]{1,0:T(8,128)(2,1)S(1)} %pad_maximum_fusion.15), channel_id=1, source_target_pairs={{0,24},{4,28},{8,0},{12,4},{16,8},{20,12},{24,16},{28,20},{1,25},{... | collective-permute-start | bytes 331784 | tf_op jit(solution)/shard_map/ppermute | solution.py:80
  18.5 11.1 %collective-permute-start.14 = (bf16[96,1056]{1,0:T(8,128)(2,1)S(1)}, bf16[96,1056]{1,0:T(8,128)(2,1)S(1)}, u32[]{:S(2)}, u32[]{:S(2)}) collective-permute-start(bf16[96,1056]{1,0:T(8,128)(2,1)S(1)} %concatenate.35), channel_id=1, source_target_pairs={{0,8},{4,12},{8,16},{12,20},{16,24},{20,28},{24,0},{28,4},{1,9},{5... | collective-permute-start | bytes 608264 | tf_op jit(solution)/shard_map/ppermute | solution.py:80
  22.8 15.1 %collective-permute-start.15 = (bf16[96,1056]{1,0:T(8,128)(2,1)S(1)}, bf16[96,1056]{1,0:T(8,128)(2,1)S(1)}, u32[]{:S(2)}, u32[]{:S(2)}) collective-permute-start(bf16[96,1056]{1,0:T(8,128)(2,1)S(1)} %concatenate.35), channel_id=1, source_target_pairs={{0,16},{4,20},{8,24},{12,28},{16,0},{20,4},{24,8},{28,12},{1,17},{... | collective-permute-start | bytes 608264 | tf_op jit(solution)/shard_map/ppermute | solution.py:80
  24.4 15.0 %collective-permute-start.16 = (bf16[96,1056]{1,0:T(8,128)(2,1)S(1)}, bf16[96,1056]{1,0:T(8,128)(2,1)S(1)}, u32[]{:S(2)}, u32[]{:S(2)}) collective-permute-start(bf16[96,1056]{1,0:T(8,128)(2,1)S(1)} %concatenate.35), channel_id=1, source_target_pairs={{0,24},{4,28},{8,0},{12,4},{16,8},{20,12},{24,16},{28,20},{1,25},{... | collective-permute-start | bytes 608264 | tf_op jit(solution)/shard_map/ppermute | solution.py:80
  28.0 44.0 %collective-permute-start = (bf16[512,768]{1,0:T(8,128)(2,1)S(1)}, bf16[512,768]{1,0:T(8,128)(2,1)}, u32[]{:S(2)}, u32[]{:S(2)}) collective-permute-start(bf16[512,768]{1,0:T(8,128)(2,1)S(1)} %copy-done), channel_id=1, source_target_pairs={{0,1},{1,0},{2,3},{3,2},{4,5},{5,4},{6,7},{7,6},{8,9},{9,8},{10,11... | collective-permute-start | bytes 2359304 | tf_op jit(solution)/shard_map/ppermute | solution.py:67
  28.1 73.5 %collective-permute-start.13 = (bf16[512,768]{1,0:T(8,128)(2,1)}, bf16[512,768]{1,0:T(8,128)(2,1)}, u32[]{:S(2)}, u32[]{:S(2)}) collective-permute-start(bf16[512,768]{1,0:T(8,128)(2,1)} %dy_own.3), channel_id=1, source_target_pairs={{0,1},{1,0},{2,3},{3,2},{4,5},{5,4},{6,7},{7,6},{8,9},{9,8},{10,11... | collective-permute-start | bytes 2359304 | tf_op jit(solution)/shard_map/ppermute | solution.py:67
  39.6 16.7 %collective-permute-start.17 = (bf16[4,48,1056]{2,1,0:T(8,128)(2,1)S(1)}, bf16[4,48,1056]{2,1,0:T(8,128)(2,1)S(1)}, u32[]{:S(2)}, u32[]{:S(2)}) collective-permute-start(bf16[4,48,1056]{2,1,0:T(8,128)(2,1)S(1)} %get-tuple-element.206.za), channel_id=1, source_target_pairs={{0,4},{4,0},{8,12},{12,8},{16,20},{20,16},{24,28},{28,24},{1,5},{5... | collective-permute-start | bytes 1216520 | tf_op jit(solution)/shard_map/ppermute | solution.py:75
  40.3 17.7 %collective-permute-start.19 = (bf16[4,48,1056]{2,1,0:T(8,128)(2,1)S(1)}, bf16[4,48,1056]{2,1,0:T(8,128)(2,1)S(1)}, u32[]{:S(2)}, u32[]{:S(2)}) collective-permute-start(bf16[4,48,1056]{2,1,0:T(8,128)(2,1)S(1)} %get-tuple-element.204.zb), channel_id=1, source_target_pairs={{0,2},{1,3},{2,0},{3,1},{4,6},{5,7},{6,4},{7,5},{8,10},{9,11},{10,... | collective-permute-start | bytes 1216520 | tf_op jit(solution)/shard_map/ppermute | solution.py:71
  46.8 17.8 %collective-permute-start.11 = (bf16[2,4,48,576]{3,2,1,0:T(8,128)(2,1)S(1)}, bf16[2,4,48,576]{3,2,1,0:T(8,128)(2,1)S(1)}, u32[]{:S(2)}, u32[]{:S(2)}) collective-permute-start(bf16[2,4,48,576]{3,2,1,0:T(8,128)(2,1)S(1)} %pad_maximum_fusion.6), channel_id=1, source_target_pairs={{0,4},{4,0},{8,12},{12,8},{16,20},{20,16},{24,28},{28,24},{1,5},{5... | collective-permute-start | bytes 1327112 | tf_op jit(solution)/shard_map/ppermute | solution.py:75
  56.3 14.2 %collective-permute-start.9 = (bf16[2,4,48,576]{3,2,1,0:T(8,128)(2,1)S(1)}, bf16[2,4,48,576]{3,2,1,0:T(8,128)(2,1)S(1)}, u32[]{:S(2)}, u32[]{:S(2)}) collective-permute-start(bf16[2,4,48,576]{3,2,1,0:T(8,128)(2,1)S(1)} %pad_maximum_fusion.5), channel_id=1, source_target_pairs={{0,2},{1,3},{2,0},{3,1},{4,6},{5,7},{6,4},{7,5},{8,10},{9,11},{10,... | collective-permute-start | bytes 1327112 | tf_op jit(solution)/shard_map/ppermute | solution.py:71
  57.9 37.1 %collective-permute-start.18 = (bf16[2,4,48,1056]{3,2,1,0:T(8,128)(2,1)S(1)}, bf16[2,4,48,1056]{3,2,1,0:T(8,128)(2,1)S(1)}, u32[]{:S(2)}, u32[]{:S(2)}) collective-permute-start(bf16[2,4,48,1056]{3,2,1,0:T(8,128)(2,1)S(1)} %pad_maximum_fusion.1), channel_id=1, source_target_pairs={{0,2},{1,3},{2,0},{3,1},{4,6},{5,7},{6,4},{7,5},{8,10},{9,11},{10,... | collective-permute-start | bytes 2433032 | tf_op jit(solution)/shard_map/ppermute | solution.py:71
  64.6 30.4 %collective-permute-start.20 = (bf16[2,4,48,1056]{3,2,1,0:T(8,128)(2,1)S(1)}, bf16[2,4,48,1056]{3,2,1,0:T(8,128)(2,1)S(1)}, u32[]{:S(2)}, u32[]{:S(2)}) collective-permute-start(bf16[2,4,48,1056]{3,2,1,0:T(8,128)(2,1)S(1)} %pad_maximum_fusion.2), channel_id=1, source_target_pairs={{0,4},{4,0},{8,12},{12,8},{16,20},{20,16},{24,28},{28,24},{1,5},{5... | collective-permute-start | bytes 2433032 | tf_op jit(solution)/shard_map/ppermute | solution.py:75
  130.8 17.7 %collective-permute-start.41 = (bf16[2,4,48,864]{3,2,1,0:T(8,128)(2,1)}, bf16[2,4,48,864]{3,2,1,0:T(8,128)(2,1)S(1)}, u32[]{:S(2)}, u32[]{:S(2)}) collective-permute-start(bf16[2,4,48,864]{3,2,1,0:T(8,128)(2,1)} %get-tuple-element.109), channel_id=1, source_target_pairs={{0,4},{4,0},{8,12},{12,8},{16,20},{20,16},{24,28},{28,24},{1,5},{5... | collective-permute-start | bytes 1990664 | tf_op jit(solution)/shard_map/ppermute | solution.py:75
  132.3 19.8 %collective-permute-start.39 = (bf16[2,4,48,864]{3,2,1,0:T(8,128)(2,1)S(1)}, bf16[2,4,48,864]{3,2,1,0:T(8,128)(2,1)S(1)}, u32[]{:S(2)}, u32[]{:S(2)}) collective-permute-start(bf16[2,4,48,864]{3,2,1,0:T(8,128)(2,1)S(1)} %get-tuple-element.107), channel_id=1, source_target_pairs={{0,2},{1,3},{2,0},{3,1},{4,6},{5,7},{6,4},{7,5},{8,10},{9,11},{10,... | collective-permute-start | bytes 1990664 | tf_op jit(solution)/shard_map/ppermute | solution.py:71
  133.8 36.6 %collective-permute-start.22 = (bf16[512,768]{1,0:T(8,128)(2,1)S(1)}, bf16[512,768]{1,0:T(8,128)(2,1)}, u32[]{:S(2)}, u32[]{:S(2)}) collective-permute-start(bf16[512,768]{1,0:T(8,128)(2,1)S(1)} %get-tuple-element.79), channel_id=1, source_target_pairs={{0,1},{1,0},{2,3},{3,2},{4,5},{5,4},{6,7},{7,6},{8,9},{9,8},{10,11... | collective-permute-start | bytes 2359304 | tf_op jit(solution)/shard_map/ppermute | solution.py:67
  161.3 25.8 %collective-permute-start.23 = (bf16[1024,768]{1,0:T(8,128)(2,1)}, bf16[1024,768]{1,0:T(8,128)(2,1)}, u32[]{:S(2)}, u32[]{:S(2)}) collective-permute-start(bf16[1024,768]{1,0:T(8,128)(2,1)} %get-tuple-element.82), channel_id=1, source_target_pairs={{0,1},{1,0},{2,3},{3,2},{4,5},{5,4},{6,7},{7,6},{8,9},{9,8},{10,11... | collective-permute-start | bytes 4718600 | tf_op jit(solution)/shard_map/ppermute | solution.py:67
  166.5 15.1 %collective-permute-start.44 = (bf16[96,864]{1,0:T(8,128)(2,1)S(1)}, bf16[96,864]{1,0:T(8,128)(2,1)S(1)}, u32[]{:S(2)}, u32[]{:S(2)}) collective-permute-start(bf16[96,864]{1,0:T(8,128)(2,1)S(1)} %get-tuple-element.199), channel_id=1, source_target_pairs={{0,16},{4,20},{8,24},{12,28},{16,0},{20,4},{24,8},{28,12},{1,17},{... | collective-permute-start | bytes 497672 | tf_op jit(solution)/shard_map/ppermute | solution.py:80
  170.3 11.2 %collective-permute-start.45 = (bf16[96,864]{1,0:T(8,128)(2,1)S(1)}, bf16[96,864]{1,0:T(8,128)(2,1)S(1)}, u32[]{:S(2)}, u32[]{:S(2)}) collective-permute-start(bf16[96,864]{1,0:T(8,128)(2,1)S(1)} %get-tuple-element.198), channel_id=1, source_target_pairs={{0,24},{4,28},{8,0},{12,4},{16,8},{20,12},{24,16},{28,20},{1,25},{... | collective-permute-start | bytes 497672 | tf_op jit(solution)/shard_map/ppermute | solution.py:80
  198.5 28.2 %collective-permute-start.34 = (bf16[2,4,48,192]{3,2,1,0:T(8,128)(2,1)S(1)}, bf16[2,4,48,192]{3,2,1,0:T(8,128)(2,1)S(1)}, u32[]{:S(2)}, u32[]{:S(2)}) collective-permute-start(bf16[2,4,48,192]{3,2,1,0:T(8,128)(2,1)S(1)} %get-tuple-element.101), channel_id=1, source_target_pairs={{0,4},{4,0},{8,12},{12,8},{16,20},{20,16},{24,28},{28,24},{1,5},{5... | collective-permute-start | bytes 442376 | tf_op jit(solution)/shard_map/ppermute | solution.py:75
  199.1 29.2 %collective-permute-start.32 = (bf16[2,4,48,192]{3,2,1,0:T(8,128)(2,1)S(1)}, bf16[2,4,48,192]{3,2,1,0:T(8,128)(2,1)S(1)}, u32[]{:S(2)}, u32[]{:S(2)}) collective-permute-start(bf16[2,4,48,192]{3,2,1,0:T(8,128)(2,1)S(1)} %get-tuple-element.99), channel_id=1, source_target_pairs={{0,2},{1,3},{2,0},{3,1},{4,6},{5,7},{6,4},{7,5},{8,10},{9,11},{10,... | collective-permute-start | bytes 442376 | tf_op jit(solution)/shard_map/ppermute | solution.py:71
  225.1 32.5 %collective-permute-start.27 = (bf16[2,4,48,576]{3,2,1,0:T(8,128)(2,1)S(1)}, bf16[2,4,48,576]{3,2,1,0:T(8,128)(2,1)}, u32[]{:S(2)}, u32[]{:S(2)}) collective-permute-start(bf16[2,4,48,576]{3,2,1,0:T(8,128)(2,1)S(1)} %get-tuple-element.96), channel_id=1, source_target_pairs={{0,4},{4,0},{8,12},{12,8},{16,20},{20,16},{24,28},{28,24},{1,5},{5... | collective-permute-start | bytes 1327112 | tf_op jit(solution)/shard_map/ppermute | solution.py:75
  228.4 11.4 %collective-permute-start.33 = (bf16[4,48,192]{2,1,0:T(8,128)(2,1)S(1)}, bf16[4,48,192]{2,1,0:T(8,128)(2,1)S(1)}, u32[]{:S(2)}, u32[]{:S(2)}) collective-permute-start(bf16[4,48,192]{2,1,0:T(8,128)(2,1)S(1)} %slice_bitcast_fusion.21), channel_id=1, source_target_pairs={{0,4},{4,0},{8,12},{12,8},{16,20},{20,16},{24,28},{28,24},{1,5},{5... | collective-permute-start | bytes 221192 | tf_op jit(solution)/shard_map/ppermute | solution.py:75
  239.8 13.1 %collective-permute-start.36 = (bf16[96,192]{1,0:T(8,128)(2,1)S(1)}, bf16[96,192]{1,0:T(8,128)(2,1)S(1)}, u32[]{:S(2)}, u32[]{:S(2)}) collective-permute-start(bf16[96,192]{1,0:T(8,128)(2,1)S(1)} %get-tuple-element.225), channel_id=1, source_target_pairs={{0,8},{4,12},{8,16},{12,20},{16,24},{20,28},{24,0},{28,4},{1,9},{5... | collective-permute-start | bytes 110600 | tf_op jit(solution)/shard_map/ppermute | solution.py:80
  252.9 22.7 %collective-permute-start.24 = (bf16[512,768]{1,0:T(8,128)(2,1)}, bf16[512,768]{1,0:T(8,128)(2,1)S(1)}, u32[]{:S(2)}, u32[]{:S(2)}) collective-permute-start(bf16[512,768]{1,0:T(8,128)(2,1)} %get-tuple-element.89), channel_id=1, source_target_pairs={{0,1},{1,0},{2,3},{3,2},{4,5},{5,4},{6,7},{7,6},{8,9},{9,8},{10,11... | collective-permute-start | bytes 2359304 | tf_op jit(solution)/shard_map/ppermute | solution.py:67
  252.9 14.2 %collective-permute-start.25 = (bf16[2,4,48,576]{3,2,1,0:T(8,128)(2,1)S(1)}, bf16[2,4,48,576]{3,2,1,0:T(8,128)(2,1)}, u32[]{:S(2)}, u32[]{:S(2)}) collective-permute-start(bf16[2,4,48,576]{3,2,1,0:T(8,128)(2,1)S(1)} %get-tuple-element.94), channel_id=1, source_target_pairs={{0,2},{1,3},{2,0},{3,1},{4,6},{5,7},{6,4},{7,5},{8,10},{9,11},{10,... | collective-permute-start | bytes 1327112 | tf_op jit(solution)/shard_map/ppermute | solution.py:71
  258.8 13.0 %collective-permute-start.28 = (bf16[4,48,576]{2,1,0:T(8,128)(2,1)S(1)}, bf16[4,48,576]{2,1,0:T(8,128)(2,1)S(1)}, u32[]{:S(2)}, u32[]{:S(2)}) collective-permute-start(bf16[4,48,576]{2,1,0:T(8,128)(2,1)S(1)} %slice_bitcast_fusion.4), channel_id=1, source_target_pairs={{0,2},{1,3},{2,0},{3,1},{4,6},{5,7},{6,4},{7,5},{8,10},{9,11},{10,... | collective-permute-start | bytes 663560 | tf_op jit(solution)/shard_map/ppermute | solution.py:71
  279.2 12.4 %collective-permute-start.30 = (bf16[96,576]{1,0:T(8,128)(2,1)S(1)}, bf16[96,576]{1,0:T(8,128)(2,1)S(1)}, u32[]{:S(2)}, u32[]{:S(2)}) collective-permute-start(bf16[96,576]{1,0:T(8,128)(2,1)S(1)} %get-tuple-element.202), channel_id=1, source_target_pairs={{0,16},{4,20},{8,24},{12,28},{16,0},{20,4},{24,8},{28,12},{1,17},{... | collective-permute-start | bytes 331784 | tf_op jit(solution)/shard_map/ppermute | solution.py:80
  (49 other events, 421.6 us)

commit v2 on v1

--- a/solution.py
+++ b/solution.py
@@ -27,6 +27,7 @@
 ROWS = 256
 PAIR = 2 * HD
 VMEM_BYTES = 52 << 20
+SPARE = 64
 
 
 def dot(left, right, left_dim, right_dim):
@@ -86,9 +87,76 @@
     return count == 8
 
 
-def assemble_kernel(widths, place_ref, za, xa, ya, zb, yb, xb, *outs):
+def after(array, *others):
+    return lax.optimization_barrier((array, *others))[0]
+
+
+ANY = pl.BlockSpec(memory_space=pl.ANY)
+LOCAL = pl.BlockSpec(memory_space=pltpu.VMEM)
+SCALAR = pl.BlockSpec(memory_space=pltpu.SMEM)
+
+
+def call(kernel, name, ins, shapes, later=(), place=None, scratch=(), cost=0):
+    head = [] if place is None else [place]
+    lead, skip = len(head), len(later)
+
+    def body(*refs):
+        kernel(*refs[: lead + len(ins)], *refs[lead + len(ins) + skip :])
+
+    return pl.pallas_call(
+        body,
+        in_specs=[SCALAR] * lead + [LOCAL] * len(ins) + [ANY] * skip,
+        out_specs=[LOCAL] * len(shapes),
+        out_shape=shapes,
+        scratch_shapes=list(scratch),
+        compiler_params=params(),
+        cost_estimate=pl.CostEstimate(
+            flops=cost, bytes_accessed=sum(2 * array.size for array in ins), transcendentals=0
+        ),
+        name=name,
+    )(*head, *ins, *later)
+
+
+def like(shape, kind=low):
+    return jax.ShapeDtypeStruct(shape, kind)
+
+
+def pack_kernel(w_qkv, gains, shard, padded):
+    rows = w_qkv.shape[1]
+    padded[...] = jnp.zeros_like(padded)
+    padded[0 : gains.shape[0], 0:rows] = gains[...]
+    columns = padded[...].T[0:rows, 0:2]
+    high = columns.astype(low)
+    rest = columns - high.astype(full)
+    middle = rest.astype(low)
+    last = (rest - middle.astype(full)).astype(low)
+    filler = jnp.zeros((rows, SPARE - 6), full)
+    pieces = [w_qkv[part] for part in range(3)]
+    shard[...] = jnp.concatenate(
+        pieces + [high.astype(full), middle.astype(full), last.astype(full), filler], axis=1
+    ).astype(low)
+
+
+def pack(w_qkv, gains):
+    rows, width = w_qkv.shape[1:]
+    return call(
+        pack_kernel,
+        "pack",
+        [w_qkv, gains],
+        [like((rows, 3 * width + SPARE))],
+        scratch=[pltpu.VMEM((128, 128), full)],
+    )[0]
+
+
+def unpack_gains(columns):
+    wide = jnp.concatenate([columns.astype(full), jnp.zeros(columns.shape, full)], axis=1).T
+    return wide[0:2] + wide[2:4] + wide[4:6]
+
+
+def assemble_kernel(widths, with_gains, place_ref, za, xa, ya, zb, yb, xb, *outs):
     place = place_ref[0]
     half = za.shape[1]
+    total = sum(widths)
     for jx in range(2):
         for jz in range(4):
             source = (place // 2 + 4 - jz) % 4 * 2 + (place % 2 + jx) % 2
@@ -104,147 +172,170 @@
                         [own[:, offset : offset + width], other[:, offset : offset + width]], axis=1
                     )
                     offset += width
-
-
-def gather_weights(parts, count):
-    widths = [part.shape[1] for part in parts]
-    shard = jnp.concatenate(parts, axis=1)
-    height, total = shard.shape
-    if not staged(count):
-        own = lax.all_gather(shard, "dp", axis=0, tiled=True)
-        other = y_swap(own)
-        gathered, offset = [], 0
-        for width in widths:
-            gathered.append(
-                jnp.concatenate(
-                    [own[:, offset : offset + width], other[:, offset : offset + width]], axis=1
-                )
-            )
-            offset += width
-        return gathered
-    half = height // 2
-    along_z = [shard] + [z_shift(shard, count, step) for step in (1, 2, 3)]
-    za = jnp.stack([piece[:half] for piece in along_z])
-    zb = jnp.stack([piece[half:] for piece in along_z])
-    xa = x_swap(za, count)
-    yb = y_swap(zb)
-    ya = y_swap(jnp.stack([za, xa]))
-    xb = x_swap(jnp.stack([zb, yb]), count)
+                if with_gains:
+                    outs[-1][pl.ds(start, half), :] = own[:, total : total + SPARE]
+    if with_gains:
+        outs[-2][...] = unpack_gains(outs[-1][...])
+
+
+def assemble(pieces, widths, depth, with_gains=False):
     place = lax.axis_index("dp").astype(jnp.int32)[None]
-    return pl.pallas_call(
-        functools.partial(assemble_kernel, widths),
-        in_specs=[pl.BlockSpec(memory_space=pltpu.SMEM)]
-        + [pl.BlockSpec(memory_space=pltpu.VMEM)] * 6,
-        out_specs=[pl.BlockSpec(memory_space=pltpu.VMEM)] * len(widths),
-        out_shape=[jax.ShapeDtypeStruct((height * count, 2 * width), low) for width in widths],
-        compiler_params=params(),
-        name="assemble",
-    )(place, za, xa, ya, zb, yb, xb)
-
-
-def weight_grad_kernel(pairs, sources, fast, place_ref, *refs):
-    ins, outs, scratch = refs[: sources], refs[sources : sources + 4], refs[sources + 4 :]
+    shapes = [like((depth, 2 * width)) for width in widths]
+    scratch = []
+    if with_gains:
+        shapes.append(like((2, depth), full))
+        scratch.append(pltpu.VMEM((depth, SPARE), low))
+    return call(
+        functools.partial(assemble_kernel, widths, with_gains),
+        "assemble",
+        pieces,
+        shapes,
+        place=place,
+        scratch=scratch,
+        cost=1 << 31,
+    )
+
+
+def gathered_plainly(shard, widths, with_gains=False):
+    own = lax.all_gather(shard, "dp", axis=0, tiled=True)
+    other = y_swap(own)
+    results, offset = [], 0
+    for width in widths:
+        lanes = slice(offset, offset + width)
+        results.append(jnp.concatenate([own[:, lanes], other[:, lanes]], axis=1))
+        offset += width
+    if with_gains:
+        results.append(unpack_gains(own[:, offset : offset + SPARE]))
+    return results
+
+
+def weight_grad_kernel(pairs, halves, fast, with_gains, ins, place_ref, refs):
+    outs, scratch = refs[: 2 * halves], refs[2 * halves :]
     place = place_ref[0]
-    for (left, right), held in zip(pairs, scratch):
-        held[...] = dot(ins[left][...], ins[right][...], 0, 0)
+    sums = None
+    for index, (left, right) in enumerate(pairs):
+        parts = [ins[at][...] for at in right]
+        right_rows = parts[0] if len(parts) == 1 else jnp.concatenate(parts, axis=1)
+        grad = dot(ins[left][...], right_rows, 0, 0)
+        scratch[index][...] = grad
+        if with_gains:
+            weight = ins[with_gains[index]][...].astype(full)
+            part = jnp.sum(weight * grad, axis=1, keepdims=True)
+            sums = part if sums is None else sums + part
+    if with_gains:
+        scratch[len(pairs)][...] = jnp.broadcast_to(sums, (sums.shape[0], 128))
+    held = scratch[: len(pairs)]
+
+    def split(rows):
+        own, other = [], []
+        for array in held:
+            values = array[rows, :]
+            width = values.shape[1] // 2
+            own.append(values[:, :width])
+            other.append(values[:, width:])
+        if with_gains:
+            column = scratch[len(pairs)][rows, :][:, :SPARE]
+            own.append(column)
+            other.append(column)
+        return [jnp.concatenate(side, axis=1).astype(low) for side in (own, other)]
+
     if not fast:
-        offset = 0
-        for held in scratch:
-            width = held.shape[1] // 2
-            outs[0][:, offset : offset + width] = held[:, :width].astype(low)
-            outs[1][:, offset : offset + width] = held[:, width:].astype(low)
-            offset += width
+        outs[0][...], outs[1][...] = split(slice(None))
         return
-    ay, by, ax, bx = outs
-    half = ay.shape[2]
+    size = outs[0].shape[2]
     for jx in range(2):
         for jz in range(4):
             target = (place // 2 + jz) % 4 * 2 + (place % 2 + jx) % 2
-            for part in range(2):
-                start = pl.multiple_of(target * 2 * half + part * half, half)
-                own, other = [], []
-                for held in scratch:
-                    width = held.shape[1] // 2
-                    rows = held[pl.ds(start, half), :].astype(low)
-                    own.append(rows[:, :width])
-                    other.append(rows[:, width:])
-                own = jnp.concatenate(own, axis=1)
-                other = jnp.concatenate(other, axis=1)
-                if part == 0:
-                    ay[jx, jz] = own
-                    by[jx, jz] = other
+            for part in range(halves):
+                start = pl.multiple_of((target * halves + part) * size, size)
+                own, other = split(pl.ds(start, size))
+                if fast == "y" or (fast == "both" and part == 0):
+                    outs[0][jx, jz] = own
+                    outs[1][jx, jz] = other
                 else:
-                    (ax, bx)[jx][0, jz] = own
-                    (ax, bx)[jx][1, jz] = other
-
-
-def reduced_weight_grad(arrays, pairs, count):
+                    outs[2 * part + jx][0, jz] = own
+                    outs[2 * part + jx][1, jz] = other
+
+
+def weight_grad(arrays, pairs, count, order, weights=(), later=()):
     depth = arrays[pairs[0][0]].shape[1]
-    widths = [arrays[right].shape[1] for _, right in pairs]
-    total = sum(widths) // 2
-    fast = staged(count)
+    widths = [sum(arrays[at].shape[1] for at in right) for _, right in pairs]
+    total = sum(widths) // 2 + (SPARE if weights else 0)
+    fast = order if staged(count) else None
+    halves = 2 if fast == "both" else 1
     if fast:
-        half = depth // count // 2
-        outs = [jax.ShapeDtypeStruct((2, 4, half, total), low)] * 4
+        shapes = [like((2, 4, depth // count // halves, total))] * (2 * halves)
     else:
-        outs = [jax.ShapeDtypeStruct((depth, total), low)] * 2 + [
-            jax.ShapeDtypeStruct((8, 128), low)
-        ] * 2
+        shapes = [like((depth, total))] * 2
     place = lax.axis_index("dp").astype(jnp.int32)[None]
-    flops = 2 * depth * sum(widths) * L
-    first, second, third, fourth = pl.pallas_call(
-        functools.partial(weight_grad_kernel, pairs, len(arrays), fast),
-        in_specs=[pl.BlockSpec(memory_space=pltpu.SMEM)]
-        + [pl.BlockSpec(memory_space=pltpu.VMEM)] * len(arrays),
-        out_specs=[pl.BlockSpec(memory_space=pltpu.VMEM)] * 4,
-        out_shape=outs,
-        scratch_shapes=[pltpu.VMEM((depth, width), full) for width in widths],
-        compiler_params=params(),
-        cost_estimate=pl.CostEstimate(
-            flops=flops, bytes_accessed=4 * depth * sum(widths), transcendentals=0
-        ),
-        name="weight_grad",
-    )(place, *arrays)
-    if not fast:
-        summed = first.astype(full) + y_swap(second).astype(full)
-        return lax.psum_scatter(summed, "dp", scatter_dimension=0, tiled=True)
-
-    def add(here, there):
-        return (here.astype(full) + there.astype(full)).astype(low)
-
-    from_y = y_swap(second)
-    from_x = x_swap(fourth, count)
-    part_a = add(first, from_y)
-    part_b = add(third, from_x)
-    next_a = x_swap(part_a[1], count)
-    next_b = y_swap(part_b[1])
-    merged = jnp.concatenate([add(part_a[0], next_a), add(part_b[0], next_b)], axis=1)
-    result = merged[0].astype(full)
-    for step in (1, 2, 3):
-        result = result + z_shift(merged[step], count, step).astype(full)
-    return result
-
-
-def sum_everywhere(array, count):
-    array = array + core_swap(array)
-    array = array + y_swap(array)
-    if not staged(count):
-        return lax.psum(array, "dp")
-    array = array + x_swap(array, count)
-    return array + sum(z_shift(array, count, step) for step in (1, 2, 3))
-
-
-def gather_gains(gains, count):
-    if not staged(count):
-        return lax.all_gather(gains, "dp", axis=1, tiled=True)
-    along_z = jnp.stack([gains] + [z_shift(gains, count, step) for step in (1, 2, 3)])
-    pieces = jnp.concatenate([along_z, x_swap(along_z, count)])
-    place = lax.axis_index("dp")
-    order = np.arange(count)
-    sources = (place // 2 + 4 - order % 4) % 4 * 2 + (place % 2 + order // 4) % 2
-    chosen = sources[:, None] == order[None, :]
-    spread = jnp.where(chosen[:, :, None, None], pieces[:, None], 0.0).sum(axis=0)
-    return spread.transpose(1, 0, 2).reshape(gains.shape[0], -1)
+    ins = list(arrays) + list(weights)
+    with_gains = tuple(range(len(arrays), len(ins)))
+    held = [pltpu.VMEM((depth, width), full) for width in widths]
+    if weights:
+        held.append(pltpu.VMEM((depth, 128), full))
+
+    def kernel(place_ref, *refs):
+        weight_grad_kernel(
+            pairs, halves, fast, with_gains, refs[: len(ins)], place_ref, refs[len(ins) :]
+        )
+
+    return call(
+        kernel,
+        "weight_grad",
+        ins,
+        shapes,
+        later=later,
+        place=place,
+        scratch=held,
+        cost=6 * depth * sum(widths) * L,
+    )
+
+
+def reduced_plainly(own, other):
+    summed = own.astype(full) + y_swap(other).astype(full)
+    return [lax.psum_scatter(summed, "dp", scatter_dimension=0, tiled=True)]
+
+
+def add_kernel(*refs):
+    groups = len(refs) // 4
+    for at in range(groups):
+        here, there = refs[2 * at : 2 * at + 2]
+        stay, go = refs[2 * groups + 2 * at : 2 * groups + 2 * at + 2]
+        stay[...] = (here[0].astype(full) + there[0].astype(full)).astype(low)
+        go[...] = (here[1].astype(full) + there[1].astype(full)).astype(low)
+
+
+def add_first(pairs, later=()):
+    shapes = [like(here.shape[1:]) for here, _ in pairs for _ in range(2)]
+    flat = [array for pair in pairs for array in pair]
+    return call(add_kernel, "add_first", flat, shapes, later=later, cost=1 << 30)
+
+
+def merge_kernel(axis, here_a, there_a, here_b, there_b, *outs):
+    for step, out in enumerate(outs):
+        part_a = here_a[step].astype(full) + there_a[step].astype(full)
+        part_b = here_b[step].astype(full) + there_b[step].astype(full)
+        out[...] = jnp.concatenate([part_a, part_b], axis=axis).astype(low)
+
+
+def add_second(here_a, there_a, here_b, there_b, axis, later=()):
+    _, rows, width = here_a.shape
+    if axis == 0:
+        shape = (2 * rows, width)
+    else:
+        shape = (rows, width + here_b.shape[2])
+    return call(
+        functools.partial(merge_kernel, axis),
+        "add_second",
+        [here_a, there_a, here_b, there_b],
+        [like(shape)] * 4,
+        later=later,
+        cost=1 << 30,
+    )
+
+
+def across_z(parts, count):
+    return [parts[0]] + [z_shift(parts[step], count, step) for step in (1, 2, 3)]
 
 
 def normalized(values):
@@ -259,9 +350,7 @@
     inner = grads * scales
     mean_inner = jnp.mean(inner, axis=-1, keepdims=True)
     mean_unit = jnp.mean(inner * unit, axis=-1, keepdims=True)
-    return scale * (inner - mean_inner - unit * mean_unit), jnp.sum(
-        grads * unit, axis=0, keepdims=True
-    )
+    return scale * (inner - mean_inner - unit * mean_unit)
 
 
 def rope_tables(offset):
@@ -405,24 +494,28 @@
     dv_out[...] = dv[...].astype(low)
 
 
-def attend_back(query, key, value, mixed, grad, lse, cosine, sine):
-    width = query.shape[1]
-    pairs = width // PAIR
-    block = pl.BlockSpec((L, PAIR), lambda i: (0, i))
-    totals = pl.BlockSpec((1, 2, L), lambda i: (i, 0, 0))
+def attend_back(pair, query, key, value, mixed, grad, lse, cosine, sine, later=()):
+    block = pl.BlockSpec((L, PAIR), lambda i: (0, pair))
+    result = pl.BlockSpec((L, PAIR), lambda i: (0, 0))
+    totals = pl.BlockSpec((1, 2, L), lambda i: (pair, 0, 0))
+    skip = len(later)
+
+    def body(*refs):
+        attend_back_kernel(*refs[:8], *refs[8 + skip :])
+
     return pl.pallas_call(
-        attend_back_kernel,
-        grid=(pairs,),
-        in_specs=[block] * 5 + [totals] + [whole((L, PAIR))] * 2,
-        out_specs=[block] * 3,
-        out_shape=[jax.ShapeDtypeStruct((L, width), low)] * 3,
+        body,
+        grid=(1,),
+        in_specs=[block] * 5 + [totals] + [whole((L, PAIR))] * 2 + [ANY] * skip,
+        out_specs=[result] * 3,
+        out_shape=[like((L, PAIR))] * 3,
         scratch_shapes=[pltpu.VMEM((L, PAIR), full)] * 2,
         compiler_params=params(),
         cost_estimate=pl.CostEstimate(
-            flops=40 * L * L * width, bytes_accessed=16 * L * width, transcendentals=2 * pairs * L * L
+            flops=60 * L * L * PAIR, bytes_accessed=16 * L * PAIR, transcendentals=2 * L * L
         ),
         name="attend_back",
-    )(query, key, value, mixed, grad, lse, cosine, sine)
+    )(query, key, value, mixed, grad, lse, cosine, sine, *later)
 
 
 def feed_forward_kernel(
@@ -542,26 +635,19 @@
 
 
 def resid_back_kernel(
-    resid, grad_own, grad_other, dy_own, dy_other, gain, wo, dresid, dresid_low, dmixed, gain_grad
+    resid, grad_own, grad_other, dy_own, dy_other, gain, wo, dresid, dresid_low, dmixed
 ):
-    step = pl.program_id(0)
-    own = is_own(step)
+    own = is_own(pl.program_id(0))
     pull = jnp.where(own, dy_own[...], dy_other[...]).astype(full)
     grads = grad_own[...] + grad_other[...].astype(full)
-    back, gain_part = norm_back(resid[...], gain[...], grads)
-    total = pull + back
+    total = pull + norm_back(resid[...], gain[...], grads)
     rounded = total.astype(low)
     dresid_low[...] = rounded
     dmixed[...] = dot(rounded, wo[...], 1, 0).astype(low)
 
-    @pl.when(step == 0)
-    def _():
-        gain_grad[...] = jnp.zeros_like(gain_grad)
-
     @pl.when(own)
     def _():
         dresid[...] = total
-        gain_grad[...] += gain_part
 
 
 def resid_back(resid, grad_own, grad_other, dy_own, dy_other, gain, wo):
@@ -578,12 +664,11 @@
             whole((1, depth)),
             whole((depth, width)),
         ],
-        out_specs=[rows_of(depth, own_half), rows_of(depth), rows_of(width), whole((1, depth))],
+        out_specs=[rows_of(depth, own_half), rows_of(depth), rows_of(width)],
         out_shape=[
             jax.ShapeDtypeStruct((L // 2, depth), full),
             jax.ShapeDtypeStruct((L, depth), low),
             jax.ShapeDtypeStruct((L, width), low),
-            jax.ShapeDtypeStruct((1, depth), full),
         ],
         compiler_params=params(),
         cost_estimate=pl.CostEstimate(
@@ -593,10 +678,13 @@
     )(resid, grad_own, grad_other, dy_own, dy_other, gain, wo)
 
 
-def project_back_kernel(dq, dk, dv, wq, wk, wv, grad_own, grad_other):
-    grad = (
-        dot(dq[...], wq[...], 1, 1) + dot(dk[...], wk[...], 1, 1) + dot(dv[...], wv[...], 1, 1)
-    )
+def project_back_kernel(*refs):
+    grads, weights, (grad_own, grad_other) = refs[:9], refs[9:12], refs[12:14]
+    grad = None
+    for part in range(3):
+        rows = jnp.concatenate([ref[...] for ref in grads[3 * part : 3 * part + 3]], axis=1)
+        term = dot(rows, weights[part][...], 1, 1)
+        grad = term if grad is None else grad + term
     own = is_own(pl.program_id(0))
 
     @pl.when(own)
@@ -608,35 +696,30 @@
         grad_other[...] = grad.astype(low)
 
 
-def project_back(dq, dk, dv, wq, wk, wv):
+def project_back(grads, wq, wk, wv, later=()):
     depth, width = wq.shape
+    skip = len(later)
+
+    def body(*refs):
+        project_back_kernel(*refs[:12], *refs[12 + skip :])
+
     return pl.pallas_call(
-        project_back_kernel,
+        body,
         grid=(L // ROWS,),
-        in_specs=[rows_of(width)] * 3 + [whole((depth, width))] * 3,
+        in_specs=[rows_of(PAIR)] * 9 + [whole((depth, width))] * 3 + [ANY] * skip,
         out_specs=[rows_of(depth, own_half), rows_of(depth, other_half)],
-        out_shape=[
-            jax.ShapeDtypeStruct((L // 2, depth), full),
-            jax.ShapeDtypeStruct((L // 2, depth), low),
-        ],
+        out_shape=[like((L // 2, depth), full), like((L // 2, depth))],
         compiler_params=params(),
         cost_estimate=pl.CostEstimate(
-            flops=6 * L * depth * width, bytes_accessed=8 * L * depth, transcendentals=0
+            flops=18 * L * depth * width, bytes_accessed=8 * L * depth, transcendentals=0
         ),
         name="project_back",
-    )(dq, dk, dv, wq, wk, wv)
-
-
-def input_back_kernel(tokens, grad_own, grad_other, dresid, gain, result, gain_grad):
+    )(*grads, wq, wk, wv, *later)
+
+
+def input_back_kernel(tokens, grad_own, grad_other, dresid, gain, result):
     grads = grad_own[...] + grad_other[...].astype(full)
-    back, gain_part = norm_back(tokens[...].astype(full), gain[...], grads)
-    result[...] = dresid[...] + back
-
-    @pl.when(pl.program_id(0) == 0)
-    def _():
-        gain_grad[...] = jnp.zeros_like(gain_grad)
-
-    gain_grad[...] += gain_part
+    result[...] = dresid[...] + norm_back(tokens[...].astype(full), gain[...], grads)
 
 
 def input_back(tokens, grad_own, grad_other, dresid, gain):
@@ -645,11 +728,8 @@
         input_back_kernel,
         grid=(height // ROWS,),
         in_specs=[rows_of(depth)] * 4 + [whole((1, depth))],
-        out_specs=[rows_of(depth), whole((1, depth))],
-        out_shape=[
-            jax.ShapeDtypeStruct((height, depth), full),
-            jax.ShapeDtypeStruct((1, depth), full),
-        ],
+        out_specs=rows_of(depth),
+        out_shape=like((height, depth), full),
         compiler_params=params(),
         cost_estimate=pl.CostEstimate(
             flops=20 * height * depth, bytes_accessed=16 * height * depth, transcendentals=0
@@ -667,6 +747,58 @@
         / (jnp.sqrt(second_new / (1.0 - beta_two**STEP)) + adam_eps)
     )
     return (weight - rate * (step_size + decay * weight), first_new, second_new)
+
+
+def step_kernel(parts, flipped, spans, *refs):
+    pieces, rest = refs[:parts], refs[parts:]
+    count = len(spans)
+    states, outs = rest[: 3 * count], rest[3 * count : 7 * count]
+    scratch = rest[7 * count :]
+    total = pieces[0][...].astype(full)
+    for piece in pieces[1:]:
+        total = total + piece[...].astype(full)
+    rows = total.shape[0]
+    for at, span in enumerate(spans):
+        weight, first, second = states[3 * at : 3 * at + 3]
+        grad_out, weight_out, first_out, second_out = outs[4 * at : 4 * at + 4]
+        for part, (start, width) in enumerate(span):
+            grad = total[:, start : start + width]
+            if flipped[at]:
+                padded = scratch[at]
+                padded[...] = jnp.zeros_like(padded)
+                padded[0:rows, 0:width] = grad
+                grad = padded[...].T[0:width, 0:rows]
+                where = Ellipsis
+            else:
+                where = part
+            new = adamw(
+                weight[where], grad, first[where], second[where], weight_rate, weight_decay
+            )
+            grad_out[where] = grad
+            weight_out[where], first_out[where], second_out[where] = new
+
+
+def step(pieces, spans, states, flipped, later=()):
+    shapes, scratch = [], []
+    for (weight, _, _), span, flip in zip(states, spans, flipped):
+        shapes += [like(weight.shape, full)] * 4
+        lanes = -(-span[0][1] // 128) * 128
+        scratch.append(pltpu.VMEM((128, lanes) if flip else (8, 128), full))
+    flat = [array for state in states for array in state]
+    results = call(
+        functools.partial(step_kernel, len(pieces), flipped, spans),
+        "step",
+        list(pieces) + flat,
+        shapes,
+        later=later,
+        scratch=scratch,
+        cost=1 << 30,
+    )
+    return [results[4 * at : 4 * at + 4] for at in range(len(states))]
+
+
+def column(pieces, at):
+    return sum(piece[:, at : at + 1].astype(full) for piece in pieces)
 
 
 def shards(
@@ -689,25 +821,61 @@
     second_gains,
 ):
     count = lax.axis_size("dp")
+    fast = staged(count)
     core = lax.axis_index("tensor") % 2
-    place = lax.axis_index("dp")
-    x_other = core_swap(tokens)
-    gains_all = gather_gains(gains, count)
+    head_width = w_qkv.shape[2]
+    unit_width = w_in.shape[2]
+    depth = tokens.shape[1]
+    qkv_widths = [head_width] * 3
+    rest_widths = [head_width, unit_width, unit_width, unit_width]
+
+    shard_one = pack(w_qkv, gains)
+    shard_two = jnp.concatenate(
+        [
+            w_attn_out.astype(low).T,
+            w_in[0].astype(low),
+            w_in[1].astype(low),
+            w_mlp_out.astype(low).T,
+        ],
+        axis=1,
+    )
+    cosine, sine = rope_tables(core * (L // 2))
+
+    def halves(shard, along):
+        half = shard.shape[0] // 2
+        pieces = [shard] + along
+        return jnp.stack([p[:half] for p in pieces]), jnp.stack([p[half:] for p in pieces])
+
+    if fast:
+        along_one = [z_shift(shard_one, count, jump) for jump in (1, 2, 3)]
+        za, zb = halves(shard_one, along_one)
+        x_other = core_swap(after(tokens, *along_one))
+        shard_two = after(shard_two, *along_one)
+        along_two = [z_shift(shard_two, count, jump) for jump in (1, 2, 3)]
+        xa, yb = x_swap(za, count), y_swap(zb)
+        ya, xb = y_swap(jnp.stack([za, xa])), x_swap(jnp.stack([zb, yb]), count)
+        wq, wk, wv, gains_all = assemble([za, xa, ya, zb, yb, xb], qkv_widths, depth, True)
+    else:
+        x_other = core_swap(tokens)
+        wq, wk, wv, gains_all = gathered_plainly(shard_one, qkv_widths, True)
     gain_one, gain_two = gains_all[0:1], gains_all[1:2]
-    wq, wk, wv = gather_weights([w_qkv[c].astype(low) for c in range(3)], count)
-    wo, w_gate, w_up, w_down = gather_weights(
-        [w_attn_out.astype(low).T, w_in[0].astype(low), w_in[1].astype(low), w_mlp_out.astype(low).T],
-        count,
-    )
-    wo_other = core_swap(wo)
-    dy_other = core_swap(cotangent)
-    cosine, sine = rope_tables(core * (L // 2))
-
     normed_one, query, key, value = project(
         tokens, x_other, gain_one, wq, wk, wv, cosine, sine
     )
+    if fast:
+        za, zb = halves(shard_two, [after(piece, ya, xb) for piece in along_two])
+        xa, yb = after(x_swap(za, count), query), after(y_swap(zb), query)
+        ya, xb = y_swap(jnp.stack([za, xa])), x_swap(jnp.stack([zb, yb]), count)
+    dy_other = core_swap(after(cotangent, query))
     mixed, lse = attend(query, key, value)
     mixed_other = core_swap(mixed)
+    if fast:
+        ya, xb = after(ya, mixed), after(xb, mixed)
+        wo, w_gate, w_up, w_down = assemble([za, xa, ya, zb, yb, xb], rest_widths, depth)
+    else:
+        wo, w_gate, w_up, w_down = gathered_plainly(shard_two, rest_widths)
+    wo_other = core_swap(wo)
+    dy_rows = jnp.concatenate([cotangent, dy_other])
     resid, normed_two, hidden, dgate, dup, out_own, out_other, dnormed, dnormed_low = feed_forward(
         mixed,
         mixed_other,
@@ -723,62 +891,109 @@
         w_down,
     )
     dnormed_other = core_swap(dnormed_low)
+    grad_a = weight_grad(
+        [normed_two, dgate, dup], [(0, (1,)), (0, (2,))], count, "y", [w_gate, w_up]
+    )
+    if fast:
+        from_a = y_swap(grad_a[1])
+    dnormed_other = after(dnormed_other, *grad_a)
+    dresid, dresid_low, dmixed = resid_back(
+        resid, dnormed, dnormed_other, cotangent, dy_other, gain_two, wo
+    )
+    grad_b = weight_grad(
+        [dy_rows, hidden, dresid_low, mixed], [(0, (1,)), (2, (3,))], count, "x", later=[dmixed]
+    )
+    if fast:
+        from_b = x_swap(grad_b[1], count)
+    bundle = (query, key, value, mixed, dmixed, lse, cosine, sine)
+    pair_0 = attend_back(0, *bundle, later=grad_b[:1])
+    if fast:
+        stay_a, go_a = add_first([(grad_a[0], from_a)], later=pair_0[:1])
+        next_a = x_swap(go_a, count)
+        pair_1 = attend_back(1, *bundle, later=[go_a])
+        stay_b, go_b = add_first([(grad_b[0], from_b)], later=pair_1[:1])
+        next_b = y_swap(go_b)
+        pair_2 = attend_back(2, *bundle, later=[go_b])
+    else:
+        pair_1, pair_2 = attend_back(1, *bundle), attend_back(2, *bundle)
+    trios = [group[part] for part in range(3) for group in (pair_0, pair_1, pair_2)]
+    grad_c = weight_grad(
+        [normed_one, *trios],
+        [(0, (1, 2, 3)), (0, (4, 5, 6)), (0, (7, 8, 9))],
+        count,
+        "both",
+        [wq, wk, wv],
+    )
+    if fast:
+        from_y, from_x = y_swap(grad_c[1]), x_swap(grad_c[3], count)
+        merged = add_second(stay_a, next_a, stay_b, next_b, 1, later=grad_c[:1])
+        pieces_one = across_z(merged, count)
+    else:
+        first_sum = reduced_plainly(*grad_a)[0]
+        pieces_one = [jnp.concatenate([first_sum, reduced_plainly(*grad_b)[0]], axis=1)]
+    grad_one, grad_one_low = project_back(trios, wq, wk, wv, later=grad_c[:1])
+    if fast:
+        from_y, from_x = after(from_y, grad_one), after(from_x, grad_one)
+        stay_a, go_a, stay_b, go_b = add_first([(grad_c[0], from_y), (grad_c[2], from_x)])
+        next_a, next_b = x_swap(go_a, count), y_swap(go_b)
+    grad_other = core_swap(grad_one_low)
     output = (out_own + core_swap(out_other).astype(full)).astype(low)
-    dy_rows = jnp.concatenate([cotangent, dy_other])
-    grad_mlp = reduced_weight_grad(
-        [normed_two, dgate, dup, dy_rows, hidden], [(0, 1), (0, 2), (3, 4)], count
-    )
-    dresid, dresid_low, dmixed, grad_gain_two = resid_back(
-        resid, dnormed, dnormed_other, cotangent, dy_other, gain_two, wo
-    )
-    dq, dk, dv = attend_back(query, key, value, mixed, dmixed, lse, cosine, sine)
-    grad_attn = reduced_weight_grad([dresid_low, mixed], [(0, 1)], count)
-    grad_proj = reduced_weight_grad([normed_one, dq, dk, dv], [(0, 1), (0, 2), (0, 3)], count)
-    grad_one, grad_one_low = project_back(dq, dk, dv, wq, wk, wv)
-    grad_inputs, grad_gain_one = input_back(
-        tokens, grad_one, core_swap(grad_one_low), dresid, gain_one
-    )
-    grad_gains = sum_everywhere(jnp.concatenate([grad_gain_one, grad_gain_two]), count)
-
-    head_width = w_qkv.shape[2]
-    unit_width = w_in.shape[2]
-    shard_qkv = jnp.stack([grad_proj[:, c * head_width : (c + 1) * head_width] for c in range(3)])
-    shard_attn = grad_attn.T
-    shard_in = jnp.stack([grad_mlp[:, c * unit_width : (c + 1) * unit_width] for c in range(2)])
-    shard_down = grad_mlp[:, 2 * unit_width :].T
-    shard_gain = lax.dynamic_slice_in_dim(grad_gains, place * gains.shape[1], gains.shape[1], axis=1)
-
-    new_qkv = adamw(w_qkv, shard_qkv, first_qkv, second_qkv, weight_rate, weight_decay)
-    new_attn = adamw(
-        w_attn_out, shard_attn, first_attn_out, second_attn_out, weight_rate, weight_decay
-    )
-    new_in = adamw(w_in, shard_in, first_in, second_in, weight_rate, weight_decay)
-    new_down = adamw(
-        w_mlp_out, shard_down, first_mlp_out, second_mlp_out, weight_rate, weight_decay
+    grad_inputs = input_back(tokens, grad_one, grad_other, dresid, gain_one)
+    if fast:
+        next_a, next_b = after(next_a, grad_inputs, output), after(next_b, grad_inputs, output)
+        merged = add_second(stay_a, next_a, stay_b, next_b, 0)
+        pieces_two = across_z(merged, count)
+    else:
+        pieces_two = reduced_plainly(*grad_c)
+    base = 2 * unit_width + SPARE
+    new_in, new_attn, new_down = step(
+        pieces_one,
+        [
+            [(0, unit_width), (unit_width, unit_width)],
+            [(base + unit_width, head_width)],
+            [(base, unit_width)],
+        ],
+        [
+            (w_in, first_in, second_in),
+            (w_attn_out, first_attn_out, second_attn_out),
+            (w_mlp_out, first_mlp_out, second_mlp_out),
+        ],
+        (False, True, True),
+        later=merged[:1] if fast else (),
+    )
+    if fast:
+        pieces_two = [after(piece, new_in[0]) for piece in pieces_two]
+    sums = jnp.concatenate([column(pieces_two, 3 * head_width), column(pieces_one, 2 * unit_width)], 1)
+    shard_gain = (sums + core_swap(sums)).T / gains
+    (new_qkv,) = step(
+        pieces_two,
+        [[(part * head_width, head_width) for part in range(3)]],
+        [(w_qkv, first_qkv, second_qkv)],
+        (False,),
     )
     new_gain = adamw(gains, shard_gain, first_gains, second_gains, gain_rate, 0.0)
     return (
         output,
         grad_inputs,
-        shard_qkv,
-        shard_attn,
-        shard_in,
-        shard_down,
-        shard_gain,
         new_qkv[0],
         new_attn[0],
         new_in[0],
         new_down[0],
-        new_gain[0],
+        shard_gain,
         new_qkv[1],
         new_attn[1],
         new_in[1],
         new_down[1],
-        new_gain[1],
+        new_gain[0],
         new_qkv[2],
         new_attn[2],
         new_in[2],
         new_down[2],
+        new_gain[1],
+        new_qkv[3],
+        new_attn[3],
+        new_in[3],
+        new_down[3],
         new_gain[2],
     )
 

time: 308 us -> 237 us (0.77)
  waiting for transfers between devices: 90.3 us -> 34.9 us
  starting transfers between devices: 69 us -> 52.3 us
  Pallas kernels: 97.7 us -> 114 us
  other arithmetic: 22.2 us -> 10 us
  local copies, waits for them, and re-layouts: 23 us -> 19.8 us
    ppermute x12 -> x8, waiting for transfers between devices: 50.2 us -> 0.7 us  [x_swap(): return lax.ppermute(array, 'dp', [(d, d ^ 1) for d in range(count)])]
    pallas_call x7 -> x17, Pallas kernels: 47.5 us -> 63.9 us  [the longest x13 36.4 us: call(): pl.pallas_call(body, in_specs=[SCALAR] * lead + [LOCAL] * len(ins) + [ANY...]
    ppermute x11 -> x8, waiting for transfers between devices: 16.4 us -> 5.39 us  [y_swap(): return lax.ppermute(array, 'tensor', [(t, t ^ 2) for t in range(4)])]
    convert_element_type x12 -> x0, other arithmetic: 6.5 us -> none  [add(): return (here.astype(full) + there.astype(full)).astype(low)]
    ppermute x12 -> x8, starting transfers between devices: 15.5 us -> 9.25 us  [x_swap(): return lax.ppermute(array, 'dp', [(d, d ^ 1) for d in range(count)])]
    ppermute x21 -> x12, starting transfers between devices: 38.2 us -> 32.4 us  [z_shift(): lax.ppermute(array, 'dp', [(d, (d // 2 + step) % around * 2 + d % 2) for...]
    unnamed x76 -> x96, local copies, waits for them, and re-layouts: 19.8 us -> 14.9 us
    ppermute x11 -> x8, starting transfers between devices: 14.1 us -> 9.6 us  [y_swap(): return lax.ppermute(array, 'tensor', [(t, t ^ 2) for t in range(4)])]
  transfers between devices with their start and end apart: 52 -> 36, of which waited for: 19 -> 9; matrix products, arithmetic and copies ran while one was open for 12% -> 7% of each run, Pallas kernels for 19% -> 41%
where the time goes in v2:
time: 237 us; the launch traced here: 232 us
  Pallas kernels  114 us (48%)
  starting transfers between devices  52.3 us (22%)
  waiting for transfers between devices  34.9 us (15%)
  local copies, waits for them, and re-layouts  19.8 us (8%)
  other arithmetic  10 us (4%)
    pallas_call x13, Pallas kernels, call(): pl.pallas_call(body, in_specs=[SCALAR] * lead + [LOCAL] * len(ins) + [ANY...  36.4 us
    ppermute x12, starting transfers between devices, z_shift(): lax.ppermute(array, 'dp', [(d, (d // 2 + step) % around * 2 + d % 2) for...  32.4 us
    ppermute x12, waiting for transfers between devices, z_shift(): lax.ppermute(array, 'dp', [(d, (d // 2 + step) % around * 2 + d % 2) for...  26.6 us
    pallas_call x3, Pallas kernels, attend_back(): pl.pallas_call(body, grid=(1,), in_specs=[block] * 5 + [totals] + [whole(...  21.5 us
    pallas_call x1, Pallas kernels, feed_forward(): pl.pallas_call(feed_forward_kernel, grid=(L // ROWS,), in_specs=[rows_of(...  18.3 us
    unnamed x96, local copies, waits for them, and re-layouts  14.9 us
    pallas_call x1, Pallas kernels, attend(): pl.pallas_call(attend_kernel, grid=(pairs,), in_specs=[block] * 3, out_sp...  13.9 us
    ppermute x8, starting transfers between devices, y_swap(): return lax.ppermute(array, 'tensor', [(t, t ^ 2) for t in range(4)])  9.6 us
  transfers between devices with their start and end apart: 36, of which 9 were waited for; matrix products, arithmetic and copies ran while one was open for 7% of the time, Pallas kernels for 41%

profile of v2, /device:TPU:0, one launch (start us, length us, event | category | flops | bytes accessed | tf_op | source)
XLA Modules:
  0.0 232.5 jit_solution(4106496127116088666)
XLA Ops:
  2.5 3.1 %collective-permute-start = (bf16[96,640]{1,0:T(8,128)(2,1)S(1)}, bf16[96,640]{1,0:T(8,128)(2,1)S(1)}, u32[]{:S(2)}, u32[]{:S(2)}) collective-permute-start(bf16[96,640]{1,0:T(8,128)(2,1)S(1)} %pack.1), channel_id=1, source_target_pairs={{0,8},{4,12},{8,16},{12,20},{16,24},{20,28},{24,0},{28,4},{1,9},{5... | collective-permute-start | bytes 368648 | tf_op jit(solution)/shard_map/ppermute | solution.py:81
  5.6 2.6 %collective-permute-start.1 = (bf16[96,640]{1,0:T(8,128)(2,1)S(1)}, bf16[96,640]{1,0:T(8,128)(2,1)S(1)}, u32[]{:S(2)}, u32[]{:S(2)}) collective-permute-start(bf16[96,640]{1,0:T(8,128)(2,1)S(1)} %pack.1), channel_id=1, source_target_pairs={{0,16},{4,20},{8,24},{12,28},{16,0},{20,4},{24,8},{28,12},{1,17},{... | collective-permute-start | bytes 368648 | tf_op jit(solution)/shard_map/ppermute | solution.py:81
  10.5 1.9 fusion
  12.5 3.8 %collective-permute-done.1 = bf16[96,640]{1,0:T(8,128)(2,1)S(1)} collective-permute-done((bf16[96,640]{1,0:T(8,128)(2,1)S(1)}, bf16[96,640]{1,0:T(8,128)(2,1)S(1)}, u32[]{:S(2)}, u32[]{:S(2)}) %collective-permute-start.1) | collective-permute-done | bytes 122912 | tf_op jit(solution)/shard_map/ppermute | solution.py:81
  20.2 4.0 %collective-permute-done.6.refs_5_ = bf16[4,48,640]{2,1,0:T(8,128)(2,1)S(1)} collective-permute-done((bf16[4,48,640]{2,1,0:T(8,128)(2,1)S(1)}, bf16[4,48,640]{2,1,0:T(8,128)(2,1)S(1)}, u32[]{:S(2)}, u32[]{:S(2)}) %collective-permute-start.6) | collective-permute-done | bytes 245792 | tf_op jit(solution)/shard_map/ppermute | solution.py:72
  33.1 2.1 collective-permute-start.11
  35.3 3.4 %collective-permute-start.12 = (bf16[96,1056]{1,0:T(8,128)(2,1)}, bf16[96,1056]{1,0:T(8,128)(2,1)S(1)}, u32[]{:S(2)}, u32[]{:S(2)}) collective-permute-start(bf16[96,1056]{1,0:T(8,128)(2,1)} %concatenate.17), channel_id=1, source_target_pairs={{0,24},{4,28},{8,0},{12,4},{16,8},{20,12},{24,16},{28,20},{1,25},{... | collective-permute-start | bytes 608264 | tf_op jit(solution)/shard_map/ppermute | solution.py:81
  39.8 9.4 %collective-permute-done.11 = bf16[96,1056]{1,0:T(8,128)(2,1)S(1)} collective-permute-done((bf16[96,1056]{1,0:T(8,128)(2,1)}, bf16[96,1056]{1,0:T(8,128)(2,1)S(1)}, u32[]{:S(2)}, u32[]{:S(2)}) %collective-permute-start.11) | collective-permute-done | bytes 202784 | tf_op jit(solution)/shard_map/ppermute | solution.py:81
  49.2 3.2 %collective-permute-done.10 = bf16[96,1056]{1,0:T(8,128)(2,1)S(1)} collective-permute-done((bf16[96,1056]{1,0:T(8,128)(2,1)}, bf16[96,1056]{1,0:T(8,128)(2,1)S(1)}, u32[]{:S(2)}, u32[]{:S(2)}) %collective-permute-start.10) | collective-permute-done | bytes 202784 | tf_op jit(solution)/shard_map/ppermute | solution.py:81
  53.8 2.7 %assemble.2 = (bf16[768,384]{1,0:T(8,128)(2,1)}, bf16[768,384]{1,0:T(8,128)(2,1)}, bf16[768,384]{1,0:T(8,128)(2,1)}, f32[2,768]{1,0:T(2,128)S(1)}) custom-call(s32[1]{0:T(128)} %bitcast.refs_0_, bf16[4,48,640]{2,1,0:T(8,128)(2,1)S(1)} %get-tuple-element.247.refs_1_, bf16[4,48,640]{2,1,0:T(8,128)(2,1)S(1)} %collective-permute-done.4.refs_2_, ...), custom_call_target="tpu_custom_call" | custom-call | flops 2147483648 | bytes 1966080 | tf_op jit(solution)/shard_map/assemble/pallas_call | solution.py:106
  58.5 6.9 %project.1 = (bf16[1024,768]{1,0:T(8,128)(2,1)}, bf16[1024,384]{1,0:T(8,128)(2,1)}, bf16[1024,384]{1,0:T(8,128)(2,1)}, bf16[1024,384]{1,0:T(8,128)(2,1)}) custom-call(bf16[512,768]{1,0:T(8,128)(2,1)} %tokens.1, bf16[512,768]{1,0:T(8,128)(2,1)} %copy-done.42, f32[1,768]{1,0:T(1,128)S(1)} %get-tuple-element.267.gain, bf16[768,384]{1,0:T(8,128)(2,1)S(1)} %copy-done.25, ...), custom_call_target="tpu_custom_call" | custom-call | flops 1811939328 | bytes 6291456 | tf_op jit(solution)/shard_map/project/pallas_call | solution.py:393
  68.7 13.9 %attend.1 = (bf16[1024,384]{1,0:T(8,128)(2,1)S(1)}, f32[3,2,1024]{2,1,0:T(2,128)S(1)}) custom-call(bf16[1024,384]{1,0:T(8,128)(2,1)S(1)} %copy-done.24, bf16[1024,384]{1,0:T(8,128)(2,1)} %get-tuple-element.124.k_ref.refs_1_, bf16[1024,384]{1,0:T(8,128)(2,1)} %get-tuple-element.125.v_ref.refs_2_), custom_call_target="tpu_custom_call" | custom-call | flops 6442450944 | bytes 3145728 | tf_op jit(solution)/shard_map/attend/pallas_call | solution.py:446
  86.2 4.1 %assemble.3 = (bf16[768,384]{1,0:T(8,128)(2,1)}, bf16[768,576]{1,0:T(8,128)(2,1)}, bf16[768,576]{1,0:T(8,128)(2,1)}, bf16[768,576]{1,0:T(8,128)(2,1)}) custom-call(s32[1]{0:T(128)} %bitcast.refs_0_, bf16[4,48,1056]{2,1,0:T(8,128)(2,1)S(1)} %get-tuple-element.243.refs_1_, bf16[4,48,1056]{2,1,0:T(8,128)(2,1)S(1)} %collective-permute-done.13.refs_2_, ...), custom_call_target="tpu_custom_call" | custom-call | flops 2147483648 | bytes 3244032 | tf_op jit(solution)/shard_map/assemble/pallas_call | solution.py:106
  90.4 2.2 collective-permute-done.17.wo_other
  93.6 18.3 %feed_forward.1 = (f32[1024,768]{1,0:T(8,128)}, bf16[1024,768]{1,0:T(8,128)(2,1)}, bf16[1024,576]{1,0:T(8,128)(2,1)}, bf16[1024,576]{1,0:T(8,128)(2,1)}, bf16[10...) custom-call(bf16[1024,384]{1,0:T(8,128)(2,1)} %copy-done.11, ...), custom_call_target="tpu_custom_call" | custom-call | flops 6643777536 | bytes 18874368 | tf_op jit(solution)/shard_map/feed_forward/pallas_call | solution.py:588
  112.2 2.4 %pad_maximum_fusion.refs_1_ = bf16[1024,768]{1,0:T(8,128)(2,1)} fusion(bf16[512,768]{1,0:T(8,128)(2,1)} %copy-done.34, bf16[512,768]{1,0:T(8,128)(2,1)S(1)} %copy-done.33), kind=kLoop, calls=%fused_computation | loop fusion | flops 3145728 | bytes 3145728 | tf_op jit(solution)/shard_map/concatenate | solution.py:878
  114.6 5.8 %weight_grad.3 = (bf16[2,4,96,640]{3,2,1,0:T(8,128)(2,1)S(1)}, bf16[2,4,96,640]{3,2,1,0:T(8,128)(2,1)S(1)}) custom-call(s32[1]{0:T(128)} %bitcast.refs_0_, bf16[1024,768]{1,0:T(8,128)(2,1)} %get-tuple-element.145.refs_1_, bf16[1024,576]{1,0:T(8,128)(2,1)} %get-tuple-element.146.refs_2_, bf16[1024,576]{1,0:T(8,128)(2,1)} %get-tuple-element.147.refs_3_, ...), custom_call_target="tpu_custom_call" | custom-call | flops 5435817984 | bytes 5701632 | tf_op jit(solution)/shard_map/weight_grad/pallas_call | solution.py:106
  123.2 7.5 %resid_back.1 = (f32[512,768]{1,0:T(8,128)}, bf16[1024,768]{1,0:T(8,128)(2,1)}, bf16[1024,384]{1,0:T(8,128)(2,1)S(1)}) custom-call(f32[1024,768]{1,0:T(8,128)} %get-tuple-element.142.resid, f32[1024,768]{1,0:T(8,128)} %get-tuple-element.143.grad_own, bf16[1024,768]{1,0:T(8,128)(2,1)} %copy-done.36, bf16[512,768]{1,0:T(8,128)(2,1)} %dy_own.3, ...), custom_call_target="tpu_custom_call" | custom-call | flops 603979776 | bytes 12582912 | tf_op jit(solution)/shard_map/resid_back/pallas_call | solution.py:655
  131.6 5.0 %weight_grad.4 = (bf16[2,4,96,480]{3,2,1,0:T(8,128)(2,1)S(1)}, bf16[2,4,96,480]{3,2,1,0:T(8,128)(2,1)S(1)}) custom-call(s32[1]{0:T(128)} %bitcast.refs_0_, bf16[1024,768]{1,0:T(8,128)(2,1)} %pad_maximum_fusion.refs_1_, bf16[1024,576]{1,0:T(8,128)(2,1)} %get-tuple-element.153.refs_2_, bf16[1024,768]{1,0:T(8,128)(2,1)} %get-tuple-element.154.refs_3_, ...), custom_call_target="tpu_custom_call" | custom-call | flops 4529848320 | bytes 5111808 | tf_op jit(solution)/shard_map/weight_grad/pallas_call | solution.py:106
  138.5 7.0 %attend_back.3 = (bf16[1024,128]{1,0:T(8,128)(2,1)S(1)}, bf16[1024,128]{1,0:T(8,128)(2,1)S(1)}, bf16[1024,128]{1,0:T(8,128)(2,1)S(1)}) custom-call(bf16[1024,384]{1,0:T(8,128)(2,1)} %get-tuple-element.123.q_ref.refs_0_, bf16[1024,384]{1,0:T(8,128)(2,1)} %get-tuple-element.124.k_ref.refs_1_, bf16[1024,384]{1,0:T(8,128)(2,1)} %get-tuple-element.125.v_ref.refs_2_, ...), custom_call_target="tpu_custom_call" | custom-call | flops 8053063680 | bytes 2097152 | tf_op jit(solution)/shard_map/attend_back/pallas_call | solution.py:506
  150.0 7.3 %attend_back.4 = (bf16[1024,128]{1,0:T(8,128)(2,1)S(1)}, bf16[1024,128]{1,0:T(8,128)(2,1)S(1)}, bf16[1024,128]{1,0:T(8,128)(2,1)S(1)}) custom-call(bf16[1024,384]{1,0:T(8,128)(2,1)} %get-tuple-element.123.q_ref.refs_0_, bf16[1024,384]{1,0:T(8,128)(2,1)} %get-tuple-element.124.k_ref.refs_1_, bf16[1024,384]{1,0:T(8,128)(2,1)} %get-tuple-element.125.v_ref.refs_2_, ...), custom_call_target="tpu_custom_call" | custom-call | flops 8053063680 | bytes 2097152 | tf_op jit(solution)/shard_map/attend_back/pallas_call | solution.py:506
  160.3 7.2 %attend_back.5 = (bf16[1024,128]{1,0:T(8,128)(2,1)S(1)}, bf16[1024,128]{1,0:T(8,128)(2,1)S(1)}, bf16[1024,128]{1,0:T(8,128)(2,1)S(1)}) custom-call(bf16[1024,384]{1,0:T(8,128)(2,1)} %get-tuple-element.123.q_ref.refs_0_, bf16[1024,384]{1,0:T(8,128)(2,1)} %get-tuple-element.124.k_ref.refs_1_, bf16[1024,384]{1,0:T(8,128)(2,1)} %get-tuple-element.125.v_ref.refs_2_, ...), custom_call_target="tpu_custom_call" | custom-call | flops 8053063680 | bytes 2097152 | tf_op jit(solution)/shard_map/attend_back/pallas_call | solution.py:506
  168.7 6.4 %weight_grad.5 = (bf16[2,4,48,640]{3,2,1,0:T(8,128)(2,1)}, bf16[2,4,48,640]{3,2,1,0:T(8,128)(2,1)}, bf16[2,4,48,640]{3,2,1,0:T(8,128)(2,1)}, bf16[2,4,48,640]{3,2,1,0:T(8,128)(2,1)}) custom-call(s32[1]{0:T(128)} %bitcast.refs_0_, bf16[1024,768]{1,0:T(8,128)(2,1)} %get-tuple-element.168.refs_1_, bf16[1024,128]{1,0:T(8,128)(2,1)S(1)} %get-tuple-element.156.refs_2_.refs_0_, ...), custom_call_target="tpu_custom_call" | custom-call | flops 5435817984 | bytes 5701632 | tf_op jit(solution)/shard_map/weight_grad/pallas_call | solution.py:106
  177.6 6.1 %project_back.1 = (f32[512,768]{1,0:T(8,128)}, bf16[512,768]{1,0:T(8,128)(2,1)}) custom-call(bf16[1024,128]{1,0:T(8,128)(2,1)S(1)} %get-tuple-element.156.refs_2_.refs_0_, bf16[1024,128]{1,0:T(8,128)(2,1)S(1)} %get-tuple-element.158.refs_2_.refs_3_.refs_1_, bf16[1024,128]{1,0:T(8,128)(2,1)S(1)} %get-tuple-element.161.refs_4_.refs_2_, ...), custom_call_target="tpu_custom_call" | custom-call | flops 5435817984 | bytes 6291456 | tf_op jit(solution)/shard_map/project_back/pallas_call | solution.py:706
  184.5 2.0 add_second.3
  186.6 4.7 %collective-permute-start.29 = (bf16[96,1120]{1,0:T(8,128)(2,1)S(1)}, bf16[96,1120]{1,0:T(8,128)(2,1)S(1)}, u32[]{:S(2)}, u32[]{:S(2)}) collective-permute-start(bf16[96,1120]{1,0:T(8,128)(2,1)S(1)} %get-tuple-element.188), channel_id=1, source_target_pairs={{0,8},{4,12},{8,16},{12,20},{16,24},{20,28},{24,0},{28,4},{1,9},{5... | collective-permute-start | bytes 645128 | tf_op jit(solution)/shard_map/ppermute | solution.py:81
  191.2 3.3 %collective-permute-start.30 = (bf16[96,1120]{1,0:T(8,128)(2,1)}, bf16[96,1120]{1,0:T(8,128)(2,1)S(1)}, u32[]{:S(2)}, u32[]{:S(2)}) collective-permute-start(bf16[96,1120]{1,0:T(8,128)(2,1)} %get-tuple-element.189), channel_id=1, source_target_pairs={{0,16},{4,20},{8,24},{12,28},{16,0},{20,4},{24,8},{28,12},{1,17},{... | collective-permute-start | bytes 645128 | tf_op jit(solution)/shard_map/ppermute | solution.py:81
  200.9 5.0 %collective-permute-done.30.refs_2_ = bf16[96,1120]{1,0:T(8,128)(2,1)S(1)} collective-permute-done((bf16[96,1120]{1,0:T(8,128)(2,1)}, bf16[96,1120]{1,0:T(8,128)(2,1)S(1)}, u32[]{:S(2)}, u32[]{:S(2)}) %collective-permute-start.30) | collective-permute-done | bytes 215072 | tf_op jit(solution)/shard_map/ppermute | solution.py:81
  206.2 3.4 %input_back.1 = f32[512,768]{1,0:T(8,128)} custom-call(bf16[512,768]{1,0:T(8,128)(2,1)S(1)} %copy-done.1, f32[512,768]{1,0:T(8,128)} %get-tuple-element.170.grad_own, bf16[512,768]{1,0:T(8,128)(2,1)S(1)} %collective-permute-done.22.grad_other, f32[512,768]{1,0:T(8,128)} %get-tuple-element.172.dresid, f32[1,768]{1,0:T(1,128)S(1)} %get-tuple-element.267.gain), custom_call_target="tpu_custom_call" | custom-call | flops 7864320 | bytes 6291456 | tf_op jit(solution)/shard_map/input_back/pallas_call | solution.py:727
  210.8 9.5 %collective-permute-start.34 = (bf16[96,640]{1,0:T(8,128)(2,1)S(1)}, bf16[96,640]{1,0:T(8,128)(2,1)S(1)}, u32[]{:S(2)}, u32[]{:S(2)}) collective-permute-start(bf16[96,640]{1,0:T(8,128)(2,1)S(1)} %get-tuple-element.197), channel_id=1, source_target_pairs={{0,24},{4,28},{8,0},{12,4},{16,8},{20,12},{24,16},{28,20},{1,25},{... | collective-permute-start | bytes 368648 | tf_op jit(solution)/shard_map/ppermute | solution.py:81
  221.0 3.1 %step.2 = (f32[2,96,288]{2,1,0:T(8,128)}, f32[2,96,288]{2,1,0:T(8,128)}, f32[2,96,288]{2,1,0:T(8,128)}, f32[2,96,288]{2,1,0:T(8,128)}, f32[192,96]{1,0:T(8,128)}...) custom-call(bf16[96,1120]{1,0:T(8,128)(2,1)S(1)} %get-tuple-element., ...), custom_call_target="tpu_custom_call" | custom-call | flops 1073741824 | bytes 1468416 | tf_op jit(solution)/shard_map/step/pallas_call | solution.py:106
  224.5 5.3 %collective-permute-done.33.refs_2_ = bf16[96,640]{1,0:T(8,128)(2,1)S(1)} collective-permute-done((bf16[96,640]{1,0:T(8,128)(2,1)S(1)}, bf16[96,640]{1,0:T(8,128)(2,1)S(1)}, u32[]{:S(2)}, u32[]{:S(2)}) %collective-permute-start.33) | collective-permute-done | bytes 122912 | tf_op jit(solution)/shard_map/ppermute | solution.py:81
  (203 shorter events, 58.5 us)
Async XLA Ops:
  2.5 10.0 %collective-permute-start = (bf16[96,640]{1,0:T(8,128)(2,1)S(1)}, bf16[96,640]{1,0:T(8,128)(2,1)S(1)}, u32[]{:S(2)}, u32[]{:S(2)}) collective-permute-start(bf16[96,640]{1,0:T(8,128)(2,1)S(1)} %pack.1), channel_id=1, source_target_pairs={{0,8},{4,12},{8,16},{12,20},{16,24},{20,28},{24,0},{28,4},{1,9},{5... | collective-permute-start | bytes 368648 | tf_op jit(solution)/shard_map/ppermute | solution.py:81
  5.6 10.7 %collective-permute-start.1 = (bf16[96,640]{1,0:T(8,128)(2,1)S(1)}, bf16[96,640]{1,0:T(8,128)(2,1)S(1)}, u32[]{:S(2)}, u32[]{:S(2)}) collective-permute-start(bf16[96,640]{1,0:T(8,128)(2,1)S(1)} %pack.1), channel_id=1, source_target_pairs={{0,16},{4,20},{8,24},{12,28},{16,0},{20,4},{24,8},{28,12},{1,17},{... | collective-permute-start | bytes 368648 | tf_op jit(solution)/shard_map/ppermute | solution.py:81
  8.2 8.1 %collective-permute-start.2 = (bf16[96,640]{1,0:T(8,128)(2,1)S(1)}, bf16[96,640]{1,0:T(8,128)(2,1)S(1)}, u32[]{:S(2)}, u32[]{:S(2)}) collective-permute-start(bf16[96,640]{1,0:T(8,128)(2,1)S(1)} %pack.1), channel_id=1, source_target_pairs={{0,24},{4,28},{8,0},{12,4},{16,8},{20,12},{24,16},{28,20},{1,25},{... | collective-permute-start | bytes 368648 | tf_op jit(solution)/shard_map/ppermute | solution.py:81
  16.4 7.8 %collective-permute-start.6 = (bf16[4,48,640]{2,1,0:T(8,128)(2,1)S(1)}, bf16[4,48,640]{2,1,0:T(8,128)(2,1)S(1)}, u32[]{:S(2)}, u32[]{:S(2)}) collective-permute-start(bf16[4,48,640]{2,1,0:T(8,128)(2,1)S(1)} %get-tuple-element.245.refs_4_), channel_id=1, source_target_pairs={{0,2},{1,3},{2,0},{3,1},{4,6},{5,7},{6,4},{7,5},{8,10},{9,11},{10,... | collective-permute-start | bytes 737288 | tf_op jit(solution)/shard_map/ppermute | solution.py:72
  18.0 8.5 %collective-permute-start.4 = (bf16[4,48,640]{2,1,0:T(8,128)(2,1)S(1)}, bf16[4,48,640]{2,1,0:T(8,128)(2,1)S(1)}, u32[]{:S(2)}, u32[]{:S(2)}) collective-permute-start(bf16[4,48,640]{2,1,0:T(8,128)(2,1)S(1)} %get-tuple-element.247.refs_1_), channel_id=1, source_target_pairs={{0,4},{4,0},{8,12},{12,8},{16,20},{20,16},{24,28},{28,24},{1,5},{5... | collective-permute-start | bytes 737288 | tf_op jit(solution)/shard_map/ppermute | solution.py:76
  25.1 24.1 %collective-permute-start.7 = (bf16[2,4,48,640]{3,2,1,0:T(8,128)(2,1)}, bf16[2,4,48,640]{3,2,1,0:T(8,128)(2,1)S(1)}, u32[]{:S(2)}, u32[]{:S(2)}) collective-permute-start(bf16[2,4,48,640]{3,2,1,0:T(8,128)(2,1)} %pad_maximum_fusion.6), channel_id=1, source_target_pairs={{0,4},{4,0},{8,12},{12,8},{16,20},{20,16},{24,28},{28,24},{1,5},{5... | collective-permute-start | bytes 1474568 | tf_op jit(solution)/shard_map/ppermute | solution.py:76
  27.4 21.8 %collective-permute-start.5 = (bf16[2,4,48,640]{3,2,1,0:T(8,128)(2,1)}, bf16[2,4,48,640]{3,2,1,0:T(8,128)(2,1)}, u32[]{:S(2)}, u32[]{:S(2)}) collective-permute-start(bf16[2,4,48,640]{3,2,1,0:T(8,128)(2,1)} %pad_maximum_fusion.5), channel_id=1, source_target_pairs={{0,2},{1,3},{2,0},{3,1},{4,6},{5,7},{6,4},{7,5},{8,10},{9,11},{10,... | collective-permute-start | bytes 1474568 | tf_op jit(solution)/shard_map/ppermute | solution.py:72
  33.1 16.0 %collective-permute-start.11 = (bf16[96,1056]{1,0:T(8,128)(2,1)}, bf16[96,1056]{1,0:T(8,128)(2,1)S(1)}, u32[]{:S(2)}, u32[]{:S(2)}) collective-permute-start(bf16[96,1056]{1,0:T(8,128)(2,1)} %concatenate.17), channel_id=1, source_target_pairs={{0,16},{4,20},{8,24},{12,28},{16,0},{20,4},{24,8},{28,12},{1,17},{... | collective-permute-start | bytes 608264 | tf_op jit(solution)/shard_map/ppermute | solution.py:81
  35.3 13.9 %collective-permute-start.12 = (bf16[96,1056]{1,0:T(8,128)(2,1)}, bf16[96,1056]{1,0:T(8,128)(2,1)S(1)}, u32[]{:S(2)}, u32[]{:S(2)}) collective-permute-start(bf16[96,1056]{1,0:T(8,128)(2,1)} %concatenate.17), channel_id=1, source_target_pairs={{0,24},{4,28},{8,0},{12,4},{16,8},{20,12},{24,16},{28,20},{1,25},{... | collective-permute-start | bytes 608264 | tf_op jit(solution)/shard_map/ppermute | solution.py:81
  38.7 13.7 %collective-permute-start.10 = (bf16[96,1056]{1,0:T(8,128)(2,1)}, bf16[96,1056]{1,0:T(8,128)(2,1)S(1)}, u32[]{:S(2)}, u32[]{:S(2)}) collective-permute-start(bf16[96,1056]{1,0:T(8,128)(2,1)} %concatenate.17), channel_id=1, source_target_pairs={{0,8},{4,12},{8,16},{12,20},{16,24},{20,28},{24,0},{28,4},{1,9},{5... | collective-permute-start | bytes 608264 | tf_op jit(solution)/shard_map/ppermute | solution.py:81
  52.5 12.8 %collective-permute-start.15 = (bf16[4,48,1056]{2,1,0:T(8,128)(2,1)S(1)}, bf16[4,48,1056]{2,1,0:T(8,128)(2,1)S(1)}, u32[]{:S(2)}, u32[]{:S(2)}) collective-permute-start(bf16[4,48,1056]{2,1,0:T(8,128)(2,1)S(1)} %get-tuple-element.241.refs_4_), channel_id=1, source_target_pairs={{0,2},{1,3},{2,0},{3,1},{4,6},{5,7},{6,4},{7,5},{8,10},{9,11},{10,... | collective-permute-start | bytes 1216520 | tf_op jit(solution)/shard_map/ppermute | solution.py:72
  53.2 13.8 %collective-permute-start.13 = (bf16[4,48,1056]{2,1,0:T(8,128)(2,1)S(1)}, bf16[4,48,1056]{2,1,0:T(8,128)(2,1)S(1)}, u32[]{:S(2)}, u32[]{:S(2)}) collective-permute-start(bf16[4,48,1056]{2,1,0:T(8,128)(2,1)S(1)} %get-tuple-element.243.refs_1_), channel_id=1, source_target_pairs={{0,4},{4,0},{8,12},{12,8},{16,20},{20,16},{24,28},{28,24},{1,5},{5... | collective-permute-start | bytes 1216520 | tf_op jit(solution)/shard_map/ppermute | solution.py:76
  65.5 18.4 %collective-permute-start.16 = (bf16[2,4,48,1056]{3,2,1,0:T(8,128)(2,1)S(1)}, bf16[2,4,48,1056]{3,2,1,0:T(8,128)(2,1)S(1)}, u32[]{:S(2)}, u32[]{:S(2)}) collective-permute-start(bf16[2,4,48,1056]{3,2,1,0:T(8,128)(2,1)S(1)} %pad_maximum_fusion.2), channel_id=1, source_target_pairs={{0,4},{4,0},{8,12},{12,8},{16,20},{20,16},{24,28},{28,24},{1,5},{5... | collective-permute-start | bytes 2433032 | tf_op jit(solution)/shard_map/ppermute | solution.py:76
  67.1 18.2 %collective-permute-start.14 = (bf16[2,4,48,1056]{3,2,1,0:T(8,128)(2,1)S(1)}, bf16[2,4,48,1056]{3,2,1,0:T(8,128)(2,1)S(1)}, u32[]{:S(2)}, u32[]{:S(2)}) collective-permute-start(bf16[2,4,48,1056]{3,2,1,0:T(8,128)(2,1)S(1)} %pad_maximum_fusion.1), channel_id=1, source_target_pairs={{0,2},{1,3},{2,0},{3,1},{4,6},{5,7},{6,4},{7,5},{8,10},{9,11},{10,... | collective-permute-start | bytes 2433032 | tf_op jit(solution)/shard_map/ppermute | solution.py:72
  82.6 7.7 %collective-permute-start.8 = (bf16[1024,384]{1,0:T(8,128)(2,1)S(1)}, bf16[1024,384]{1,0:T(8,128)(2,1)S(1)}, u32[]{:S(2)}, u32[]{:S(2)}) collective-permute-start(bf16[1024,384]{1,0:T(8,128)(2,1)S(1)} %get-tuple-element.126.mixed_own.refs_4_.refs_3_), channel_id=1, source_target_pairs={{0,1},{1,0},{2,3},{3,2},{4,5},{5,4},{6,7},{7,6},{8,9},{9,8},{10,11... | collective-permute-start | bytes 2359304 | tf_op jit(solution)/shard_map/ppermute | solution.py:68
  112.0 10.1 %collective-permute-start.19 = (bf16[1024,768]{1,0:T(8,128)(2,1)}, bf16[1024,768]{1,0:T(8,128)(2,1)S(1)}, u32[]{:S(2)}, u32[]{:S(2)}) collective-permute-start(bf16[1024,768]{1,0:T(8,128)(2,1)} %get-tuple-element.144), channel_id=1, source_target_pairs={{0,1},{1,0},{2,3},{3,2},{4,5},{5,4},{6,7},{7,6},{8,9},{9,8},{10,11... | collective-permute-start | bytes 4718600 | tf_op jit(solution)/shard_map/ppermute | solution.py:68
  120.4 25.1 %collective-permute-start.20 = (bf16[2,4,96,640]{3,2,1,0:T(8,128)(2,1)S(1)}, bf16[2,4,96,640]{3,2,1,0:T(8,128)(2,1)S(1)}, u32[]{:S(2)}, u32[]{:S(2)}) collective-permute-start(bf16[2,4,96,640]{3,2,1,0:T(8,128)(2,1)S(1)} %get-tuple-element.149), channel_id=1, source_target_pairs={{0,2},{1,3},{2,0},{3,1},{4,6},{5,7},{6,4},{7,5},{8,10},{9,11},{10,... | collective-permute-start | bytes 2949128 | tf_op jit(solution)/shard_map/ppermute | solution.py:72
  122.0 75.7 %collective-permute-start.18 = (bf16[512,768]{1,0:T(8,128)(2,1)S(1)}, bf16[512,768]{1,0:T(8,128)(2,1)S(1)}, u32[]{:S(2)}, u32[]{:S(2)}) collective-permute-start(bf16[512,768]{1,0:T(8,128)(2,1)S(1)} %get-tuple-element.141), channel_id=1, source_target_pairs={{0,1},{1,0},{2,3},{3,2},{4,5},{5,4},{6,7},{7,6},{8,9},{9,8},{10,11... | collective-permute-start | bytes 2359304 | tf_op jit(solution)/shard_map/ppermute | solution.py:68
  137.4 20.6 %collective-permute-start.21 = (bf16[2,4,96,480]{3,2,1,0:T(8,128)(2,1)S(1)}, bf16[2,4,96,480]{3,2,1,0:T(8,128)(2,1)S(1)}, u32[]{:S(2)}, u32[]{:S(2)}) collective-permute-start(bf16[2,4,96,480]{3,2,1,0:T(8,128)(2,1)S(1)} %get-tuple-element.159), channel_id=1, source_target_pairs={{0,4},{4,0},{8,12},{12,8},{16,20},{20,16},{24,28},{28,24},{1,5},{5... | collective-permute-start | bytes 2211848 | tf_op jit(solution)/shard_map/ppermute | solution.py:76
  149.0 34.7 %collective-permute-start.27 = (bf16[4,96,640]{2,1,0:T(8,128)(2,1)S(1)}, bf16[4,96,640]{2,1,0:T(8,128)(2,1)S(1)}, u32[]{:S(2)}, u32[]{:S(2)}) collective-permute-start(bf16[4,96,640]{2,1,0:T(8,128)(2,1)S(1)} %get-tuple-element.157.refs_8_), channel_id=1, source_target_pairs={{0,4},{4,0},{8,12},{12,8},{16,20},{20,16},{24,28},{28,24},{1,5},{5... | collective-permute-start | bytes 1474568 | tf_op jit(solution)/shard_map/ppermute | solution.py:76
  168.2 15.6 %collective-permute-start.28 = (bf16[4,96,480]{2,1,0:T(8,128)(2,1)S(1)}, bf16[4,96,480]{2,1,0:T(8,128)(2,1)S(1)}, u32[]{:S(2)}, u32[]{:S(2)}) collective-permute-start(bf16[4,96,480]{2,1,0:T(8,128)(2,1)S(1)} %get-tuple-element.160.refs_8_), channel_id=1, source_target_pairs={{0,2},{1,3},{2,0},{3,1},{4,6},{5,7},{6,4},{7,5},{8,10},{9,11},{10,... | collective-permute-start | bytes 1105928 | tf_op jit(solution)/shard_map/ppermute | solution.py:72
  175.1 16.1 %collective-permute-start.24 = (bf16[2,4,48,640]{3,2,1,0:T(8,128)(2,1)}, bf16[2,4,48,640]{3,2,1,0:T(8,128)(2,1)S(1)}, u32[]{:S(2)}, u32[]{:S(2)}) collective-permute-start(bf16[2,4,48,640]{3,2,1,0:T(8,128)(2,1)} %get-tuple-element.176), channel_id=1, source_target_pairs={{0,4},{4,0},{8,12},{12,8},{16,20},{20,16},{24,28},{28,24},{1,5},{5... | collective-permute-start | bytes 1474568 | tf_op jit(solution)/shard_map/ppermute | solution.py:76
  176.2 18.4 %collective-permute-start.23 = (bf16[2,4,48,640]{3,2,1,0:T(8,128)(2,1)}, bf16[2,4,48,640]{3,2,1,0:T(8,128)(2,1)S(1)}, u32[]{:S(2)}, u32[]{:S(2)}) collective-permute-start(bf16[2,4,48,640]{3,2,1,0:T(8,128)(2,1)} %get-tuple-element.173), channel_id=1, source_target_pairs={{0,2},{1,3},{2,0},{3,1},{4,6},{5,7},{6,4},{7,5},{8,10},{9,11},{10,... | collective-permute-start | bytes 1474568 | tf_op jit(solution)/shard_map/ppermute | solution.py:72
  183.7 22.4 %collective-permute-start.22 = (bf16[512,768]{1,0:T(8,128)(2,1)}, bf16[512,768]{1,0:T(8,128)(2,1)S(1)}, u32[]{:S(2)}, u32[]{:S(2)}) collective-permute-start(bf16[512,768]{1,0:T(8,128)(2,1)} %get-tuple-element.171), channel_id=1, source_target_pairs={{0,1},{1,0},{2,3},{3,2},{4,5},{5,4},{6,7},{7,6},{8,9},{9,8},{10,11... | collective-permute-start | bytes 2359304 | tf_op jit(solution)/shard_map/ppermute | solution.py:68
  186.6 11.9 %collective-permute-start.29 = (bf16[96,1120]{1,0:T(8,128)(2,1)S(1)}, bf16[96,1120]{1,0:T(8,128)(2,1)S(1)}, u32[]{:S(2)}, u32[]{:S(2)}) collective-permute-start(bf16[96,1120]{1,0:T(8,128)(2,1)S(1)} %get-tuple-element.188), channel_id=1, source_target_pairs={{0,8},{4,12},{8,16},{12,20},{16,24},{20,28},{24,0},{28,4},{1,9},{5... | collective-permute-start | bytes 645128 | tf_op jit(solution)/shard_map/ppermute | solution.py:81
  191.2 14.6 %collective-permute-start.30 = (bf16[96,1120]{1,0:T(8,128)(2,1)}, bf16[96,1120]{1,0:T(8,128)(2,1)S(1)}, u32[]{:S(2)}, u32[]{:S(2)}) collective-permute-start(bf16[96,1120]{1,0:T(8,128)(2,1)} %get-tuple-element.189), channel_id=1, source_target_pairs={{0,16},{4,20},{8,24},{12,28},{16,0},{20,4},{24,8},{28,12},{1,17},{... | collective-permute-start | bytes 645128 | tf_op jit(solution)/shard_map/ppermute | solution.py:81
  194.5 11.4 %collective-permute-start.31 = (bf16[96,1120]{1,0:T(8,128)(2,1)}, bf16[96,1120]{1,0:T(8,128)(2,1)S(1)}, u32[]{:S(2)}, u32[]{:S(2)}) collective-permute-start(bf16[96,1120]{1,0:T(8,128)(2,1)} %get-tuple-element.190), channel_id=1, source_target_pairs={{0,24},{4,28},{8,0},{12,4},{16,8},{20,12},{24,16},{28,20},{1,25},{... | collective-permute-start | bytes 645128 | tf_op jit(solution)/shard_map/ppermute | solution.py:81
  197.7 11.9 %collective-permute-start.26 = (bf16[4,48,640]{2,1,0:T(8,128)(2,1)S(1)}, bf16[4,48,640]{2,1,0:T(8,128)(2,1)S(1)}, u32[]{:S(2)}, u32[]{:S(2)}) collective-permute-start(bf16[4,48,640]{2,1,0:T(8,128)(2,1)S(1)} %get-tuple-element.182), channel_id=1, source_target_pairs={{0,2},{1,3},{2,0},{3,1},{4,6},{5,7},{6,4},{7,5},{8,10},{9,11},{10,... | collective-permute-start | bytes 737288 | tf_op jit(solution)/shard_map/ppermute | solution.py:72
  198.5 11.1 %collective-permute-start.25 = (bf16[4,48,640]{2,1,0:T(8,128)(2,1)S(1)}, bf16[4,48,640]{2,1,0:T(8,128)(2,1)}, u32[]{:S(2)}, u32[]{:S(2)}) collective-permute-start(bf16[4,48,640]{2,1,0:T(8,128)(2,1)S(1)} %get-tuple-element.179), channel_id=1, source_target_pairs={{0,4},{4,0},{8,12},{12,8},{16,20},{20,16},{24,28},{28,24},{1,5},{5... | collective-permute-start | bytes 737288 | tf_op jit(solution)/shard_map/ppermute | solution.py:76
  210.8 13.5 %collective-permute-start.34 = (bf16[96,640]{1,0:T(8,128)(2,1)S(1)}, bf16[96,640]{1,0:T(8,128)(2,1)S(1)}, u32[]{:S(2)}, u32[]{:S(2)}) collective-permute-start(bf16[96,640]{1,0:T(8,128)(2,1)S(1)} %get-tuple-element.197), channel_id=1, source_target_pairs={{0,24},{4,28},{8,0},{12,4},{16,8},{20,12},{24,16},{28,20},{1,25},{... | collective-permute-start | bytes 368648 | tf_op jit(solution)/shard_map/ppermute | solution.py:81
  220.3 9.5 %collective-permute-start.33 = (bf16[96,640]{1,0:T(8,128)(2,1)S(1)}, bf16[96,640]{1,0:T(8,128)(2,1)S(1)}, u32[]{:S(2)}, u32[]{:S(2)}) collective-permute-start(bf16[96,640]{1,0:T(8,128)(2,1)S(1)} %get-tuple-element.195), channel_id=1, source_target_pairs={{0,16},{4,20},{8,24},{12,28},{16,0},{20,4},{24,8},{28,12},{1,17},{... | collective-permute-start | bytes 368648 | tf_op jit(solution)/shard_map/ppermute | solution.py:81
  220.3 9.7 %collective-permute-start.32 = (bf16[96,640]{1,0:T(8,128)(2,1)S(1)}, bf16[96,640]{1,0:T(8,128)(2,1)S(1)}, u32[]{:S(2)}, u32[]{:S(2)}) collective-permute-start(bf16[96,640]{1,0:T(8,128)(2,1)S(1)} %get-tuple-element.193), channel_id=1, source_target_pairs={{0,8},{4,12},{8,16},{12,20},{16,24},{20,28},{24,0},{28,4},{1,9},{5... | collective-permute-start | bytes 368648 | tf_op jit(solution)/shard_map/ppermute | solution.py:81
  (51 other events, 362.4 us)
